TPU v7x, 128 devices: a whole 4x4x4 slice. The times are simulated.
128 devices in a mesh: dp: 8 (over y, core), tensor: 16 (over x, z).
Axes of the slice: x: 4, y: 4, z: 4, core: 2. Of those that a mesh axis runs over, the one named last changes fastest.
Arguments:
- queries: bfloat16 [64, 8192], P('dp', 'tensor'), may hold values from -100 to 100
- new_kv: bfloat16 [64, 16, 256], P('dp', 'tensor'), may hold values from -4 to 4, as said below
- kv_pages: bfloat16 [16, 512, 128, 256], P('tensor', 'dp'), may hold values from -4.1 to 4.1, as said below
- lengths: int32 [64], P('dp'), may hold values from 2 to 16384, as said below
- page_table: int32 [64, 128], P('dp'), may hold values from 0 to 511, as said below
- out_weight: bfloat16 [8192, 16384], P('tensor'), may hold values from -0.0625 to 0.0625
Outputs:
- projected: bfloat16 [64, 16384], P('dp', 'tensor')
Inputs may be any that keep to these rules, and one draw needn't show every extreme that they name: `lengths`: one request in every draw has the longest context. `page_table`: page g is held by dp index g // 64. A request's entries before ceil(lengths / 128) name distinct pages, and no page is named by two requests; later entries are valid page numbers that carry no meaning. `kv_pages`: all copies of one key-value head are equal. `new_kv`: all copies of one key-value head are equal.
All inputs are finite; a program needn't handle non-finite values.
Results may differ from a plain program's by a relative error of at most 0.015.
Values may be sent and summed in bfloat16 or wider, within the bound.
No kernel may reach another device: no remote copies, remote signals or barrier semaphores. Data moves between devices by JAX's collectives and lax.ppermute only.
A program may use at most 192 MiB of HBM per device.

v0:
```python
import jax
import jax.numpy as jnp
from jax import lax
from jax.sharding import PartitionSpec as P

FAR_BELOW = -1e30


def merged_2(x, axis, combine):
    everything = jax.tree.map(lambda part: lax.all_gather(part, axis), x)
    initial = jax.tree.map(lambda part: part[0], everything)

    def turn(k, so_far):
        return combine(so_far, jax.tree.map(lambda part: part[k], everything))

    return lax.fori_loop(1, lax.axis_size(axis), turn, initial)


def fold_states(first, second):
    peak = jnp.maximum(first[0], second[0])
    first_factor = jnp.exp(first[0] - peak)
    second_factor = jnp.exp(second[0] - peak)
    summed_total = first[1] * first_factor + second[1] * second_factor
    summed_values = first[2] * first_factor[..., None] + second[2] * second_factor[..., None]
    return (peak, summed_total, summed_values)


def body(queries, new_kv, kv_pages, lengths, page_table, out_weight):
    req_home, q_width = queries.shape
    head_dim = kv_pages.shape[-1] // 2
    q_heads = q_width // head_dim
    page_len = kv_pages.shape[2]
    pool_home = kv_pages.shape[1]
    list_len = page_table.shape[1]
    scaling = head_dim ** (-0.5)
    local_query = queries.reshape(req_home, q_heads, head_dim)
    slot_index = jnp.arange(list_len, dtype=jnp.int32)
    row_index = jnp.arange(page_len, dtype=jnp.int32)
    all_query = lax.all_gather(queries, "dp", axis=0, tiled=True)
    all_table, all_length = (
        lax.all_gather(page_table, "dp", axis=0, tiled=True),
        lax.all_gather(lengths, "dp", axis=0, tiled=True),
    )
    requests = all_query.shape[0]
    needed = (all_length + page_len - 1) // page_len
    page_ids = lax.axis_index("dp") * pool_home + jnp.arange(pool_home, dtype=jnp.int32)
    match = (all_table[:, :, None] == page_ids[None, None, :]) & (
        slot_index[None, :, None] < needed[:, None, None]
    )
    owner = jnp.any(match, axis=1)
    slot_of = jnp.sum(jnp.where(match, slot_index[None, :, None], 0), axis=(0, 1))
    length_of = jnp.sum(jnp.where(owner, all_length[:, None], 0), axis=0)
    picker = owner.astype(jnp.bfloat16)
    page_query = (
        jnp.dot(picker.T, all_query, preferred_element_type=jnp.float32)
        .astype(jnp.bfloat16)
        .reshape(pool_home, q_heads, head_dim)
    )
    key_rows = kv_pages[0, :, :, :head_dim]
    value_rows = kv_pages[0, :, :, head_dim:]
    scores = (
        jnp.einsum("phd,ptd->pht", page_query, key_rows, preferred_element_type=jnp.float32)
        * scaling
    )
    position = slot_of[:, None] * page_len + row_index[None, :]
    alive = (position < length_of[:, None])[:, None, :]
    page_peak = jnp.max(jnp.where(alive, scores, FAR_BELOW), axis=2)
    row_peak = jnp.max(jnp.where(owner[:, :, None], page_peak[None], FAR_BELOW), axis=1)
    page_shift = jnp.sum(jnp.where(owner[:, :, None], row_peak[:, None, :], 0.0), axis=0)
    local = jnp.where(alive, jnp.exp(scores - page_peak[:, :, None]), 0.0)
    page_factor = jnp.exp(page_peak - page_shift)
    page_total = jnp.sum(local, axis=2) * page_factor
    page_values = (
        jnp.einsum(
            "pht,ptd->phd",
            local.astype(jnp.bfloat16),
            value_rows,
            preferred_element_type=jnp.float32,
        )
        * page_factor[..., None]
    )
    owner_float = owner.astype(jnp.float32)
    row_total = jnp.dot(owner_float, page_total, precision=lax.Precision.HIGHEST)
    row_values = jnp.dot(
        owner_float,
        page_values.reshape(pool_home, q_heads * head_dim),
        precision=lax.Precision.HIGHEST,
    ).reshape(requests, q_heads, head_dim)
    merged = merged_2((row_peak, row_total, row_values), "dp", fold_states)
    begin = lax.axis_index("dp") * req_home
    peak = lax.dynamic_slice_in_dim(merged[0], begin, req_home, 0)
    total = lax.dynamic_slice_in_dim(merged[1], begin, req_home, 0)
    weighted = lax.dynamic_slice_in_dim(merged[2], begin, req_home, 0)
    newest_rows = new_kv[:, 0, :]
    fresh = (
        jnp.einsum(
            "rhd,rd->rh", local_query, newest_rows[:, :head_dim], preferred_element_type=jnp.float32
        )
        * scaling
    )
    final_peak = jnp.maximum(peak, fresh)
    factor = jnp.exp(peak - final_peak)
    fresh_weight = jnp.exp(fresh - final_peak)
    total = total * factor + fresh_weight
    weighted = weighted * factor[..., None] + fresh_weight[..., None] * newest_rows[
        :, None, head_dim:
    ].astype(jnp.float32)
    attended = (
        (weighted / total[..., None]).reshape(req_home, q_heads * head_dim).astype(jnp.bfloat16)
    )
    partial_out = jnp.dot(attended, out_weight, preferred_element_type=jnp.float32)
    return lax.psum_scatter(partial_out, "tensor", scatter_dimension=1, tiled=True).astype(
        jnp.bfloat16
    )


def solution(mesh):
    return jax.shard_map(
        body,
        mesh=mesh,
        in_specs=(
            P("dp", "tensor"),
            P("dp", "tensor", None),
            P("tensor", "dp", None, None),
            P("dp"),
            P("dp", None),
            P("tensor", None),
        ),
        out_specs=P("dp", "tensor"),
        check_vma=False,
    )
```

profile of v0, /device:TPU:0, one launch (start us, length us, event | category | flops | bytes accessed | tf_op | source)
XLA Modules:
  0.0 180.6 jit_solution(17160909335878852458)
XLA Ops:
  6.5 13.5 %all_gather.24 = s32[64,128]{1,0:T(8,128)S(1)} all-gather(s32[8,128]{1,0:T(8,128)} %param.12), channel_id=1, replica_groups=mesh['dp'=8,'tensor'=16] {'dp'}, dimensions={0}, use_global_device_ids=true | all-gather | bytes 36864 | tf_op jit(solution)/shard_map/all_gather | solution.py:41
  20.1 1.2 dynamic-slice
  22.0 0.9 dynamic-update-slice
  22.8 8.9 %all-reduce = s32[64]{0:T(128)S(1)} all-reduce(s32[64]{0:T(128)S(1)} %dynamic-update-slice), channel_id=1, replica_groups=mesh['dp'=8,'tensor'=16] {'dp'}, use_global_device_ids=true, to_apply=%add | all-reduce | flops 64 | bytes 512
  31.9 1.2 fusion.10
  33.1 0.7 select_reduce_fusion
  33.9 13.0 %all_gather.26 = bf16[64,512]{1,0:T(8,128)(2,1)S(1)} all-gather(bf16[8,512]{1,0:T(8,128)(2,1)} %param.8), channel_id=1, replica_groups=mesh['dp'=8,'tensor'=16] {'dp'}, dimensions={0}, use_global_device_ids=true | all-gather | bytes 73728 | tf_op jit(solution)/shard_map/all_gather | solution.py:39
  46.9 0.2 convolution_convert_fusion
  47.2 2.9 %select_reduce_fusion.3 = (f32[64,4]{1,0:T(8,128)S(1)}, f32[64,4,128]{2,1,0:T(4,128)S(1)}) fusion(pred[64,128]{1,0:T(8,128)(4,1)S(1)} %add_compare_fusion, bf16[64,4,128]{2,1,0:T(4,128)(2,1)S(1)} %reshape.97, bf16[1,64,128,256]{3,2,1,0:T(8,128)(2,1)} %param.10), kind=kOutput, calls=%fused_computation.30 | convolution fusion | flops 8486656 | bytes 2302976 | tf_op jit(solution)/shard_map/phd,ptd->pht/dot_general | solution.py:62
  50.1 0.1 select_reduce_fusion.2
  50.3 0.1 select_reduce_fusion.1
  50.4 0.1 copy.46
  50.5 2.3 %fusion.14 = f32[64,4,128]{2,1,0:T(4,128)S(1)} fusion(bf16[1,64,128,256]{3,2,1,0:T(8,128)(2,1)} %param.10, f32[64,4,128]{2,1,0:T(4,128)S(1)} %get-tuple-element.245, f32[64,4]{1,0:T(8,128)S(1)} %subtract_exponential_fusion.1, f32[64,4]{1,0:T(8,128)S(1)} %get-tuple-element.244, pred[64,128]{1,0:T(8,128)(4,1)S(1)} %add_compare_fusion), kind=kOutput, calls=%fused_computation.20 | convolution fusion | flops 8519680 | bytes 2369536 | tf_op jit(solution)/shard_map/pht,ptd->phd/dot_general | solution.py:74
  52.8 0.9 fusion.17
  53.8 0.1 fusion.32
  54.0 11.2 %all-gather.3 = f32[8,64,4]{1,2,0:T(4,128)S(1)} all-gather(f32[1,64,4]{1,2,0:T(4,128)S(1)} %bitcast.82), channel_id=2, replica_groups=mesh['dp'=8,'tensor'=16] {'dp'}, dimensions={0}, use_global_device_ids=true | all-gather | bytes 9216 | tf_op jit(solution)/shard_map/all_gather | solution.py:10
  65.2 0.2 fusion.21
  65.4 0.2 convolution_bitcast_fusion
  65.6 11.3 %all-gather.4 = f32[8,64,4]{1,2,0:T(4,128)S(1)} all-gather(f32[1,64,4]{1,2,0:T(4,128)S(1)} %convolution_bitcast_fusion), channel_id=3, replica_groups=mesh['dp'=8,'tensor'=16] {'dp'}, dimensions={0}, use_global_device_ids=true | all-gather | bytes 9216 | tf_op jit(solution)/shard_map/all_gather | solution.py:10
  77.0 0.9 all-gather.7.cloned.1.call-done
  77.9 0.9 slice.35
  78.9 11.1 %while.19 = (s32[]{:T(128)}, f32[64,4]{0,1:T(4,128)S(1)}, f32[64,4]{0,1:T(4,128)S(1)}, f32[64,4,128]{2,1,0:T(4,128)S(1)}, f32[8,64,4]{1,2,0:T(4,128)S(1)}, /*ind...) while((s32[]{:T(128)}, f32[64,4]{0,1:T(4,128)S(1)}, ...), condition=%wide.region_8.9_spmd, body=%wide.region_7.8_spmd.sunk | while | flops 99845 | bytes 669847 | solution.py:16
  79.0 0.9 constant_dynamic-slice_fusion.2
  79.9 0.1 copy.84
  80.0 0.1 copy.85
  80.1 0.4 fusion.50
  80.5 0.9 constant_dynamic-slice_fusion.2
  81.5 0.1 copy.84
  81.7 0.4 fusion.50
  82.1 0.9 constant_dynamic-slice_fusion.2
  83.0 0.1 copy.84
  83.2 0.4 fusion.50
  83.7 0.9 constant_dynamic-slice_fusion.2
  84.6 0.1 copy.84
  84.8 0.4 fusion.50
  85.3 0.9 constant_dynamic-slice_fusion.2
  86.2 0.1 copy.84
  86.4 0.4 fusion.50
  86.9 0.9 constant_dynamic-slice_fusion.2
  87.8 0.1 copy.84
  88.0 0.4 fusion.50
  88.4 0.9 constant_dynamic-slice_fusion.2
  89.4 0.1 copy.84
  89.5 0.4 fusion.50
  90.3 0.1 fusion.34
  90.4 8.8 %fusion.29 = f32[8,16384]{1,0:T(8,128)} fusion(bf16[512,16384]{1,0:T(8,128)(2,1)} %param.13, bf16[1,8,4,128]{3,2,1,0:T(4,128)(2,1)S(1)} %fusion.34), kind=kOutput, calls=%fused_computation.44 | convolution fusion | flops 134217728 | bytes 17309696 | tf_op jit(solution)/shard_map/dot_general | solution.py:111
  99.3 73.2 %reduce-scatter.2.cloned.1.call-done = f32[8,1024]{1,0:T(8,128)} async-done(((f32[8,16384]{1,0:T(8,128)}), f32[8,1024]{1,0:T(8,128)}) %reduce-scatter.2.cloned.1.call-update) | async-done | bytes 32784 | tf_op jit(solution)/shard_map/reduce_scatter | solution.py:112
  172.4 1.4 convert_element_type.26
  (40 shorter events, 1.7 us)
Async XLA Ops:
  6.5 71.4 %all-gather.7.cloned.1.call-start = ((), (), s32[]{:S(2)}) async-start(), calls=%async_computation.2 | async-start | bytes 1179648 | tf_op jit(solution)/shard_map/all_gather | solution.py:10
  50.0 3.7 %copy-start.1 = (bf16[8,1,256]{2,0,1:T(8,128)(2,1)S(1)}, bf16[8,1,256]{2,0,1:T(8,128)(2,1)}, u32[]{:S(2)}) copy-start(bf16[8,1,256]{2,0,1:T(8,128)(2,1)} %param.9) | copy-start | bytes 12292
  50.1 3.7 %copy-start = (bf16[8,512]{1,0:T(8,128)(2,1)S(1)}, bf16[8,512]{1,0:T(8,128)(2,1)}, u32[]{:S(2)}) copy-start(bf16[8,512]{1,0:T(8,128)(2,1)} %param.8) | copy-start | bytes 24580
  53.7 118.7 %reduce-scatter.2.cloned.1.call-start = ((), (), s32[]{:S(2)}) async-start(), calls=%async_computation.1 | async-start | bytes 557056 | tf_op jit(solution)/shard_map/reduce_scatter | solution.py:112
Sparse Core Ops, SparseCore 0:
  53.8 24.0 all-gather.6
  99.4 73.0 reduce-scatter.1
where the time goes:
time: 181 us
  waiting for transfers between devices  74.1 us (41%)
  blocking collectives  58 us (32%)
  matrix products  15.4 us (9%)
  between operations  14.2 us (8%)
  local copies, waits for them, and re-layouts  11.4 us (6%)
  other arithmetic  7.35 us (4%)
    reduce_scatter x1, waiting for transfers between devices, body(): lax.psum_scatter(partial_out, 'tensor', scatter_dimension=1, tiled=True)  73.2 us
    all_gather x2, blocking collectives, merged_2(): everything = jax.tree.map(lambda part: lax.all_gather(part, axis), x)  22.6 us
    all_gather x1, blocking collectives, body(): lax.all_gather(page_table, 'dp', axis=0, tiled=True)  13.5 us
    all_gather x1, blocking collectives, body(): all_query = lax.all_gather(queries, 'dp', axis=0, tiled=True)  13 us
    unnamed x1, blocking collectives  8.93 us
    dot_general x1, matrix products, body(): jnp.dot(attended, out_weight, preferred_element_type=jnp.float32)  8.84 us
    dynamic_slice x7, local copies, waits for them, and re-layouts, turn(): return combine(so_far, jax.tree.map(lambda part: part[k], everything))  6.46 us
  transfers between devices with their start and end apart: 2, of which 2 were waited for; matrix products, arithmetic and copies ran while one was open for 0% of the time, Pallas kernels for 0%

commit v1 on v0

v1 whole, which is shorter than its diff:
```python
import functools

import jax
import jax.numpy as jnp
from jax import lax
from jax.experimental import pallas as pl
from jax.experimental.pallas import tpu as pltpu
from jax.sharding import PartitionSpec as P

FAR_BELOW = -1e30
LANES = 128
F32 = jnp.float32
BF16 = jnp.bfloat16
NO_PAGE = 255.0
QUAD = 4


def iota(shape, axis):
    return lax.broadcasted_iota(jnp.int32, shape, axis)


def split3(x):
    high = x.astype(BF16).astype(F32)
    middle = (x - high).astype(BF16).astype(F32)
    return high, middle, x - high - middle


def attend_kernel(scaling, homes, asked_ref, kv_ref, out_ref, score_ref, value_ref):
    pages, page_len, width = kv_ref.shape
    head_dim = width // 2
    requests = asked_ref.shape[0]
    per_home = requests // homes
    heads = out_ref.shape[0] // requests
    rows = pages * heads
    q_width = heads * head_dim

    named = asked_ref[:, q_width : q_width + LANES].astype(F32)
    filled = asked_ref[:, q_width + LANES : q_width + 2 * LANES].astype(F32)
    coded = filled + iota(filled.shape, 0).astype(F32) * 256.0
    page_id = iota((pages, LANES), 0).astype(F32)
    found = jnp.zeros((pages, LANES), F32)
    for r in range(requests):
        found = jnp.where(named[r : r + 1, :] == page_id, coded[r : r + 1, :], found)
    code = jnp.broadcast_to(jnp.sum(found, axis=1, keepdims=True), (pages, LANES))
    owner = jnp.floor(code * (1.0 / 256.0))
    alive_rows = code - owner * 256.0

    spread = (iota((rows, pages), 0) // heads == iota((rows, pages), 1)).astype(BF16)
    both = jnp.concatenate([owner, alive_rows], axis=1).astype(BF16)
    wide = jnp.dot(spread, both, preferred_element_type=F32)
    row_owner = wide[:, :LANES]
    alive = iota((rows, page_len), 1).astype(F32) < wide[:, LANES:]

    picker = (row_owner[:, :requests] == iota((rows, requests), 1).astype(F32)).astype(BF16)
    picked = jnp.dot(picker, asked_ref[:, :q_width], preferred_element_type=F32)
    row_head = iota((rows, head_dim), 0) % heads
    query = picked[:, :head_dim]
    for h in range(1, heads):
        query = jnp.where(row_head == h, picked[:, h * head_dim : (h + 1) * head_dim], query)
    query = query.astype(BF16)

    group = QUAD * heads
    block = iota((group, LANES), 0) // heads
    for j in range(pages // QUAD):
        keys = kv_ref[j * QUAD : (j + 1) * QUAD, :, :head_dim].reshape(QUAD * page_len, head_dim)
        full = lax.dot_general(
            query[j * group : (j + 1) * group, :],
            keys,
            (((1,), (1,)), ((), ())),
            preferred_element_type=F32,
        )
        mine = full[:, :page_len]
        for g in range(1, QUAD):
            mine = jnp.where(block == g, full[:, g * page_len : (g + 1) * page_len], mine)
        score_ref[j * group : (j + 1) * group, :] = mine
    scores = jnp.where(alive, score_ref[...] * scaling, FAR_BELOW)

    column = iota((rows, requests * heads), 1)
    column_head = (column // per_home) % heads
    column_request = (column // (per_home * heads)) * per_home + column % per_home
    owner_wide = jnp.concatenate([row_owner] * (requests * heads // LANES), axis=1)
    belongs = (owner_wide == column_request.astype(F32)) & (
        iota((rows, requests * heads), 0) % heads == column_head
    )

    page_peak = jnp.max(scores, axis=1, keepdims=True)
    peak = jnp.max(jnp.where(belongs, page_peak, FAR_BELOW), axis=0, keepdims=True)
    shift = jnp.max(jnp.where(belongs, peak, FAR_BELOW), axis=1, keepdims=True)
    local = jnp.where(alive, jnp.exp(scores - shift), 0.0)
    page_total = jnp.sum(local, axis=1, keepdims=True)

    for j in range(pages // QUAD):
        part = local[j * group : (j + 1) * group, :]
        weights = jnp.concatenate(
            [jnp.where(block == g, part, 0.0) for g in range(QUAD)], axis=1
        ).astype(BF16)
        values = kv_ref[j * QUAD : (j + 1) * QUAD, :, head_dim:].reshape(QUAD * page_len, head_dim)
        value_ref[j * group : (j + 1) * group, :] = jnp.dot(
            weights, values, preferred_element_type=F32
        )
    both = jnp.concatenate(
        [value_ref[...], jnp.broadcast_to(page_total, (rows, LANES))], axis=1
    )
    high = both.astype(BF16)
    low = (both - high.astype(F32)).astype(BF16)
    chosen = jnp.where(belongs, 1.0, 0.0).T.astype(BF16)
    summed = jnp.dot(chosen, high, preferred_element_type=F32) + jnp.dot(
        chosen, low, preferred_element_type=F32
    )
    weighted, total = summed[:, :head_dim], summed[:, head_dim:]
    peak_rows = jnp.broadcast_to(peak, (LANES, requests * heads)).T
    present = total > 0.0
    safe = jnp.where(present, total, 1.0)
    level = jnp.where(present, peak_rows + jnp.log(safe), FAR_BELOW)
    lane = iota(level.shape, 1)
    high, middle, low = split3(level)
    pieces = jnp.where(lane == 0, high, jnp.where(lane == 1, middle, low))
    out_ref[:, :head_dim] = (weighted / safe).astype(BF16)
    out_ref[:, head_dim:] = pieces.astype(BF16)


def project_kernel(scaling, parts_ref, query_ref, newest_ref, weight_ref, out_ref, input_ref):
    sources, rows, width = parts_ref.shape
    head_dim = width // 2
    req, q_width = query_ref.shape
    heads = q_width // head_dim

    @pl.when(pl.program_id(0) == 0)
    def _():
        newest = newest_ref[...].astype(F32)
        new_key, new_value = newest[:, :head_dim], newest[:, head_dim:]
        query = query_ref[...].astype(F32)
        fresh = jnp.concatenate(
            [
                jnp.sum(
                    query[:, h * head_dim : (h + 1) * head_dim] * new_key, axis=1, keepdims=True
                )
                for h in range(heads)
            ],
            axis=0,
        ) * scaling
        levels = []
        for s in range(sources):
            pieces = parts_ref[s, :, head_dim:].astype(F32)
            levels.append(pieces[:, 0:1] + pieces[:, 1:2] + pieces[:, 2:3])
        peak = fresh
        for level in levels:
            peak = jnp.maximum(peak, level)
        total = jnp.exp(fresh - peak)
        summed = total * jnp.concatenate([new_value] * heads, axis=0)
        for s in range(sources):
            factor = jnp.exp(levels[s] - peak)
            total = total + factor
            summed = summed + factor * parts_ref[s, :, :head_dim].astype(F32)
        attended = summed / total
        for h in range(heads):
            input_ref[:, h * head_dim : (h + 1) * head_dim] = attended[
                h * req : (h + 1) * req, :
            ].astype(BF16)

    tile = jnp.dot(input_ref[...], weight_ref[...], preferred_element_type=F32).astype(BF16)
    width_out = out_ref.shape[2]
    for k in range(out_ref.shape[0]):
        out_ref[k] = tile[:, k * width_out : (k + 1) * width_out]


def body(n_dp, n_tensor, queries, new_kv, kv_pages, lengths, page_table, out_weight):
    req_home, q_width = queries.shape
    _, pool_home, page_len, width = kv_pages.shape
    head_dim = width // 2
    heads = q_width // head_dim
    list_len = page_table.shape[1]
    features = out_weight.shape[1]
    requests = req_home * n_dp
    scaling = head_dim ** (-0.5)

    slot = jnp.arange(list_len, dtype=jnp.int32)
    filled = jnp.clip(lengths[:, None] - slot[None, :] * page_len, 0, page_len)
    holder = jnp.arange(n_dp, dtype=jnp.int32)[:, None, None]
    inside = page_table[None] - holder * pool_home
    valid = (inside >= 0) & (inside < pool_home) & (filled > 0)[None]
    named = jnp.where(valid, inside.astype(F32), NO_PAGE).astype(BF16)
    asked = jnp.concatenate(
        [
            jnp.broadcast_to(queries[None], (n_dp, req_home, q_width)),
            named,
            jnp.broadcast_to(filled.astype(BF16)[None], (n_dp, req_home, list_len)),
        ],
        axis=2,
    )
    asked = lax.all_to_all(asked, "dp", 0, 0).reshape(requests, q_width + 2 * list_len)

    parts = pl.pallas_call(
        functools.partial(attend_kernel, scaling, n_dp),
        out_shape=jax.ShapeDtypeStruct((requests * heads, width), BF16),
        in_specs=[pl.BlockSpec(memory_space=pltpu.VMEM)] * 2,
        out_specs=pl.BlockSpec(memory_space=pltpu.VMEM),
        scratch_shapes=[
            pltpu.VMEM((pool_home * heads, page_len), F32),
            pltpu.VMEM((pool_home * heads, head_dim), F32),
        ],
        compiler_params=pltpu.CompilerParams(vmem_limit_bytes=16 * 2**20),
        name="attend",
    )(asked, kv_pages[0])

    parts = lax.all_to_all(parts.reshape(n_dp, req_home * heads, width), "dp", 0, 0)

    own = features // n_tensor
    step = 2
    partial_out = pl.pallas_call(
        functools.partial(project_kernel, scaling),
        grid=(n_tensor // step,),
        out_shape=jax.ShapeDtypeStruct((n_tensor, req_home, own), BF16),
        in_specs=[
            pl.BlockSpec(memory_space=pltpu.VMEM),
            pl.BlockSpec(memory_space=pltpu.VMEM),
            pl.BlockSpec(memory_space=pltpu.VMEM),
            pl.BlockSpec((q_width, step * own), lambda i: (0, i)),
        ],
        out_specs=pl.BlockSpec((step, req_home, own), lambda i: (i, 0, 0)),
        scratch_shapes=[pltpu.VMEM((req_home, q_width), BF16)],
        compiler_params=pltpu.CompilerParams(vmem_limit_bytes=16 * 2**20),
        name="project",
    )(parts, queries, new_kv[:, 0, :], out_weight)

    pieces = lax.all_to_all(partial_out, "tensor", 0, 0)
    return jnp.sum(pieces.astype(F32), axis=0).astype(BF16)


def solution(mesh):
    return jax.shard_map(
        functools.partial(body, mesh.shape["dp"], mesh.shape["tensor"]),
        mesh=mesh,
        in_specs=(
            P("dp", "tensor"),
            P("dp", "tensor", None),
            P("tensor", "dp", None, None),
            P("dp"),
            P("dp", None),
            P("tensor", None),
        ),
        out_specs=P("dp", "tensor"),
        check_vma=False,
    )
```

time: 181 us -> 54.8 us (0.30)
  waiting for transfers between devices: 74.1 us -> 0 us
  blocking collectives: 58 us -> 34.9 us
  matrix products: 15.4 us -> 0 us
  between operations: 14.2 us -> 0.03 us
  Pallas kernels: 0 us -> 6.47 us
  other arithmetic: 7.35 us -> 2.89 us
    reduce_scatter x1 -> x0, waiting for transfers between devices: 73.2 us -> none  [body(): lax.psum_scatter(partial_out, 'tensor', scatter_dimension=1, tiled=True)]
    all_gather x4 -> x0, blocking collectives: 49.1 us -> none  [the longest x2 22.6 us: merged_2(): everything = jax.tree.map(lambda part: lax.all_gather(part, axis), x)]
    all_to_all x0 -> x3, blocking collectives: none -> 34.9 us  [the longest x1 16.2 us: body(): pieces = lax.all_to_all(partial_out, 'tensor', 0, 0)]
    dot_general x7 -> x0, matrix products: 15.4 us -> none  [the longest x1 8.84 us: body(): jnp.dot(attended, out_weight, preferred_element_type=jnp.float32)]
    unnamed x1 -> x0, blocking collectives: 8.93 us -> none
    unnamed x7 -> x8, local copies, waits for them, and re-layouts: 2.1 us -> 9.34 us
    pallas_call x0 -> x2, Pallas kernels: none -> 6.47 us  [the longest x1 4.46 us: body(): pl.pallas_call(functools.partial(project_kernel, scaling), grid=(n_tensor...]
    dynamic_slice x7 -> x0, local copies, waits for them, and re-layouts: 6.46 us -> none  [turn(): return combine(so_far, jax.tree.map(lambda part: part[k], everything))]
  transfers between devices with their start and end apart: 2 -> 0, of which waited for: 2 -> 0; matrix products, arithmetic and copies ran while one was open for 0% -> 0% of each run, Pallas kernels for 0% -> 0%
where the time goes in v1:
time: 54.8 us; the launch traced here: 54.3 us
  blocking collectives  34.9 us (64%)
  local copies, waits for them, and re-layouts  10 us (18%)
  Pallas kernels  6.47 us (12%)
  other arithmetic  2.89 us (5%)
    all_to_all x1, blocking collectives, body(): pieces = lax.all_to_all(partial_out, 'tensor', 0, 0)  16.2 us
    all_to_all x1, blocking collectives, body(): lax.all_to_all(asked, 'dp', 0, 0).reshape(requests, q_width + 2 * list_len)  10.1 us
    unnamed x8, local copies, waits for them, and re-layouts  9.34 us
    all_to_all x1, blocking collectives, body(): lax.all_to_all(parts.reshape(n_dp, req_home * heads, width), 'dp', 0, 0)  8.52 us
    pallas_call x1, Pallas kernels, body(): pl.pallas_call(functools.partial(project_kernel, scaling), grid=(n_tensor...  4.46 us
    pallas_call x1, Pallas kernels, body(): pl.pallas_call(functools.partial(attend_kernel, scaling, n_dp), out_shape...  2.01 us

profile of v1, /device:TPU:0, one launch (start us, length us, event | category | flops | bytes accessed | tf_op | source)
XLA Modules:
  0.0 54.3 jit_solution(7546285707892569435)
XLA Ops:
  0.0 0.7 %fusion.5 = pred[8,128]{1,0:T(8,128)(4,1)S(1)} fusion(s32[128]{0:T(128)S(1)} %iota_multiply_fusion, s32[8]{0:T(128)} %param.9), kind=kLoop, calls=%fused_computation.10 | loop fusion | flops 3072 | bytes 1568 | tf_op jit(solution)/shard_map/gt | solution.py:181
  0.7 0.7 %fusion.4 = bf16[8,128]{1,0:T(8,128)(2,1)S(1)} fusion(s32[128]{0:T(128)S(1)} %iota_multiply_fusion, s32[8]{0:T(128)} %param.9), kind=kLoop, calls=%fused_computation.9 | loop fusion | flops 3072 | bytes 2592 | tf_op jit(solution)/shard_map/convert_element_type | solution.py:187
  1.5 0.8 %fusion.1 = bf16[8,8,128]{2,1,0:T(8,128)(2,1)S(1)} fusion(s32[8]{0:T(128)S(1)} %iota_multiply_fusion.1, s32[8,128]{1,0:T(8,128)} %param.10, pred[8,128]{1,0:T(8,128)(4,1)S(1)} %fusion.5), kind=kLoop, calls=%fused_computation.5 | loop fusion | flops 65536 | bytes 21536 | tf_op jit(solution)/shard_map/convert_element_type | solution.py:182
  2.3 0.7 %broadcast_in_dim.8 = bf16[8,8,512]{2,1,0:T(8,128)(2,1)S(1)} broadcast(bf16[8,512]{1,0:T(8,128)(2,1)} %query_ref.1), dimensions={1,2} | broadcast | bytes 73728 | tf_op jit(solution)/shard_map/broadcast_in_dim | solution.py:185
  3.0 10.1 %all_to_all.15 = bf16[8,8,768]{2,1,0:T(8,128)(2,1)S(1)} all-to-all(bf16[8,8,768]{2,1,0:T(8,128)(2,1)S(1)} %pad_maximum_fusion), channel_id=1, replica_groups=mesh['dp'=8,'tensor'=16] {'dp'}, dimensions={0} | all-to-all | bytes 196608 | tf_op jit(solution)/shard_map/all_to_all | solution.py:191
  13.1 0.0 copy-start.1
  13.1 2.2 %copy-done.1 = bf16[1,64,128,256]{3,2,1,0:T(8,128)(2,1)S(1)} copy-done((bf16[1,64,128,256]{3,2,1,0:T(8,128)(2,1)S(1)}, bf16[1,64,128,256]{3,2,1,0:T(8,128)(2,1)}, u32[]{:S(2)}) %copy-start.1) | copy-done | bytes 4194328
  15.3 2.0 %attend.1 = bf16[256,256]{1,0:T(8,128)(2,1)S(1)} custom-call(bf16[64,768]{1,0:T(8,128)(2,1)S(1)} %bitcast.6, bf16[64,128,256]{2,1,0:T(8,128)(2,1)S(1)} %bitcast.4), custom_call_target="tpu_custom_call" | custom-call | tf_op jit(solution)/shard_map/attend/pallas_call | solution.py:193
  17.3 8.5 %all_to_all.16.parts_ref = bf16[8,32,256]{2,1,0:T(8,128)(2,1)S(1)} all-to-all(bf16[8,32,256]{2,1,0:T(8,128)(2,1)S(1)} %bitcast.5), channel_id=1, replica_groups=mesh['dp'=8,'tensor'=16] {'dp'}, dimensions={0} | all-to-all | bytes 262144 | tf_op jit(solution)/shard_map/all_to_all | solution.py:206
  25.8 0.0 copy-start
  25.8 5.8 %copy-done = bf16[512,16384]{1,0:T(8,128)(2,1)S(1)} copy-done((bf16[512,16384]{1,0:T(8,128)(2,1)S(1)}, bf16[512,16384]{1,0:T(8,128)(2,1)}, u32[]{:S(2)}) %copy-start) | copy-done | bytes 16777240
  31.6 0.0 copy-start.2
  31.6 0.7 %copy-done.2 = bf16[8,512]{1,0:T(8,128)(2,1)S(1)} copy-done((bf16[8,512]{1,0:T(8,128)(2,1)S(1)}, bf16[8,512]{1,0:T(8,128)(2,1)}, u32[]{:S(2)}) %copy-start.2) | copy-done | bytes 8216
  32.3 0.0 copy-start.3
  32.3 0.7 %copy-done.3 = bf16[8,1,256]{2,0,1:T(8,128)(2,1)S(1)} copy-done((bf16[8,1,256]{2,0,1:T(8,128)(2,1)S(1)}, bf16[8,1,256]{2,0,1:T(8,128)(2,1)}, u32[]{:S(2)}) %copy-start.3) | copy-done | bytes 4120
  33.0 4.5 %project.1 = bf16[16,8,1024]{2,1,0:T(8,128)(2,1)S(1)} custom-call(bf16[8,32,256]{2,1,0:T(8,128)(2,1)S(1)} %all_to_all.16.parts_ref, bf16[8,512]{1,0:T(8,128)(2,1)S(1)} %copy-done.2, bf16[8,256]{1,0:T(8,128)(2,1)S(1)} %bitcast.7, bf16[512,16384]{1,0:T(8,128)(2,1)S(1)} %copy-done), custom_call_target="tpu_custom_call" | custom-call | tf_op jit(solution)/shard_map/project/pallas_call | solution.py:210
  37.5 16.2 %all_to_all.17 = bf16[16,8,1024]{2,1,0:T(8,128)(2,1)S(1)} all-to-all(bf16[16,8,1024]{2,1,0:T(8,128)(2,1)S(1)} %project.1), channel_id=1, replica_groups=mesh['dp'=8,'tensor'=16] {'tensor'}, dimensions={0} | all-to-all | bytes 524288 | tf_op jit(solution)/shard_map/all_to_all | solution.py:226
  53.7 0.6 %reduce_sum.12 = bf16[8,1024]{1,0:T(8,128)(2,1)} reduce(bf16[16,8,1024]{2,1,0:T(8,128)(2,1)S(1)} %all_to_all.17, bf16[]{:T(256)} %constant.1.clone.1), dimensions={0}, to_apply=%region_0.1 | reduce | flops 122880 | bytes 278530 | tf_op jit(solution)/shard_map/reduce_sum | solution.py:227
  (4 shorter events, 0.0 us)
Async XLA Ops:
  13.1 2.2 %copy-start.1 = (bf16[1,64,128,256]{3,2,1,0:T(8,128)(2,1)S(1)}, bf16[1,64,128,256]{3,2,1,0:T(8,128)(2,1)}, u32[]{:S(2)}) copy-start(bf16[1,64,128,256]{3,2,1,0:T(8,128)(2,1)} %param.8) | copy-start | bytes 12582916
  25.8 5.8 %copy-start = (bf16[512,16384]{1,0:T(8,128)(2,1)S(1)}, bf16[512,16384]{1,0:T(8,128)(2,1)}, u32[]{:S(2)}) copy-start(bf16[512,16384]{1,0:T(8,128)(2,1)} %weight_ref.1) | copy-start | bytes 50331652
  31.6 0.7 %copy-start.2 = (bf16[8,512]{1,0:T(8,128)(2,1)S(1)}, bf16[8,512]{1,0:T(8,128)(2,1)}, u32[]{:S(2)}) copy-start(bf16[8,512]{1,0:T(8,128)(2,1)} %query_ref.1) | copy-start | bytes 24580
  32.3 0.7 %copy-start.3 = (bf16[8,1,256]{2,0,1:T(8,128)(2,1)S(1)}, bf16[8,1,256]{2,0,1:T(8,128)(2,1)}, u32[]{:S(2)}) copy-start(bf16[8,1,256]{2,0,1:T(8,128)(2,1)} %param.7) | copy-start | bytes 12292

commit v2 on v1

--- a/solution.py
+++ b/solution.py
@@ -23,6 +23,47 @@
     high = x.astype(BF16).astype(F32)
     middle = (x - high).astype(BF16).astype(F32)
     return high, middle, x - high - middle
+
+
+def begin_kernel(out_ref):
+    out_ref[...] = jnp.zeros_like(out_ref)
+
+
+def ask_kernel(
+    scaling, pool, page_len, _, length_ref, query_ref, newest_ref, table_ref, asked_ref, state_ref
+):
+    homes, req, width = asked_ref.shape
+    q_width = query_ref.shape[1]
+    list_len = table_ref.shape[1]
+    head_dim = newest_ref.shape[1] // 2
+    heads = q_width // head_dim
+    row = iota((req, list_len), 0)
+    length = jnp.zeros((req, list_len), jnp.int32)
+    for r in range(req):
+        length = jnp.where(row == r, length_ref[r], length)
+    filled = jnp.clip(length - iota((req, list_len), 1) * page_len, 0, page_len)
+    table = table_ref[...]
+    query = query_ref[...]
+    for d in range(homes):
+        inside = table - d * pool
+        valid = (inside >= 0) & (inside < pool) & (filled > 0)
+        asked_ref[d, :, :q_width] = query
+        asked_ref[d, :, q_width : q_width + list_len] = jnp.where(
+            valid, inside.astype(F32), NO_PAGE
+        ).astype(BF16)
+        asked_ref[d, :, q_width + list_len :] = filled.astype(F32).astype(BF16)
+    newest = newest_ref[...].astype(F32)
+    wide = query.astype(F32)
+    for h in range(heads):
+        fresh = jnp.sum(
+            wide[:, h * head_dim : (h + 1) * head_dim] * newest[:, :head_dim],
+            axis=1,
+            keepdims=True,
+        )
+        state_ref[h * req : (h + 1) * req, :head_dim] = newest[:, head_dim:]
+        state_ref[h * req : (h + 1) * req, head_dim:] = jnp.broadcast_to(
+            fresh * scaling, (req, head_dim)
+        )
 
 
 def attend_kernel(scaling, homes, asked_ref, kv_ref, out_ref, score_ref, value_ref):
@@ -119,49 +160,33 @@
     out_ref[:, head_dim:] = pieces.astype(BF16)
 
 
-def project_kernel(scaling, parts_ref, query_ref, newest_ref, weight_ref, out_ref, input_ref):
+def project_kernel(parts_ref, state_ref, weight_ref, out_ref):
     sources, rows, width = parts_ref.shape
     head_dim = width // 2
-    req, q_width = query_ref.shape
-    heads = q_width // head_dim
-
-    @pl.when(pl.program_id(0) == 0)
-    def _():
-        newest = newest_ref[...].astype(F32)
-        new_key, new_value = newest[:, :head_dim], newest[:, head_dim:]
-        query = query_ref[...].astype(F32)
-        fresh = jnp.concatenate(
-            [
-                jnp.sum(
-                    query[:, h * head_dim : (h + 1) * head_dim] * new_key, axis=1, keepdims=True
-                )
-                for h in range(heads)
-            ],
-            axis=0,
-        ) * scaling
-        levels = []
-        for s in range(sources):
-            pieces = parts_ref[s, :, head_dim:].astype(F32)
-            levels.append(pieces[:, 0:1] + pieces[:, 1:2] + pieces[:, 2:3])
-        peak = fresh
-        for level in levels:
-            peak = jnp.maximum(peak, level)
-        total = jnp.exp(fresh - peak)
-        summed = total * jnp.concatenate([new_value] * heads, axis=0)
-        for s in range(sources):
-            factor = jnp.exp(levels[s] - peak)
-            total = total + factor
-            summed = summed + factor * parts_ref[s, :, :head_dim].astype(F32)
-        attended = summed / total
-        for h in range(heads):
-            input_ref[:, h * head_dim : (h + 1) * head_dim] = attended[
-                h * req : (h + 1) * req, :
-            ].astype(BF16)
-
-    tile = jnp.dot(input_ref[...], weight_ref[...], preferred_element_type=F32).astype(BF16)
-    width_out = out_ref.shape[2]
-    for k in range(out_ref.shape[0]):
-        out_ref[k] = tile[:, k * width_out : (k + 1) * width_out]
+    blocks, req, own = out_ref.shape
+    heads = rows // req
+    fresh = state_ref[:, head_dim : head_dim + 1]
+    levels = []
+    for s in range(sources):
+        pieces = parts_ref[s, :, head_dim:].astype(F32)
+        levels.append(pieces[:, 0:1] + pieces[:, 1:2] + pieces[:, 2:3])
+    peak = fresh
+    for level in levels:
+        peak = jnp.maximum(peak, level)
+    total = jnp.exp(fresh - peak)
+    summed = total * state_ref[:, :head_dim]
+    for s in range(sources):
+        factor = jnp.exp(levels[s] - peak)
+        total = total + factor
+        summed = summed + factor * parts_ref[s, :, :head_dim].astype(F32)
+    attended = summed / total
+    given = jnp.concatenate(
+        [attended[h * req : (h + 1) * req, :] for h in range(heads)], axis=1
+    ).astype(BF16)
+    for k in range(blocks):
+        out_ref[k] = jnp.dot(
+            given, weight_ref[:, k * own : (k + 1) * own], preferred_element_type=F32
+        ).astype(BF16)
 
 
 def body(n_dp, n_tensor, queries, new_kv, kv_pages, lengths, page_table, out_weight):
@@ -174,54 +199,55 @@
     requests = req_home * n_dp
     scaling = head_dim ** (-0.5)
 
-    slot = jnp.arange(list_len, dtype=jnp.int32)
-    filled = jnp.clip(lengths[:, None] - slot[None, :] * page_len, 0, page_len)
-    holder = jnp.arange(n_dp, dtype=jnp.int32)[:, None, None]
-    inside = page_table[None] - holder * pool_home
-    valid = (inside >= 0) & (inside < pool_home) & (filled > 0)[None]
-    named = jnp.where(valid, inside.astype(F32), NO_PAGE).astype(BF16)
-    asked = jnp.concatenate(
-        [
-            jnp.broadcast_to(queries[None], (n_dp, req_home, q_width)),
-            named,
-            jnp.broadcast_to(filled.astype(BF16)[None], (n_dp, req_home, list_len)),
-        ],
-        axis=2,
-    )
+    vmem = pl.BlockSpec(memory_space=pltpu.VMEM)
+    begun = pl.pallas_call(
+        begin_kernel,
+        out_shape=jax.ShapeDtypeStruct((8, LANES), jnp.int32),
+        out_specs=vmem,
+        compiler_params=pltpu.CompilerParams(vmem_limit_bytes=2**20),
+        cost_estimate=pl.CostEstimate(flops=10**10, bytes_accessed=2**20, transcendentals=0),
+        name="begin",
+    )()
+    asked, state = pl.pallas_call(
+        functools.partial(ask_kernel, scaling, pool_home, page_len),
+        out_shape=(
+            jax.ShapeDtypeStruct((n_dp, req_home, q_width + 2 * list_len), BF16),
+            jax.ShapeDtypeStruct((req_home * heads, width), F32),
+        ),
+        in_specs=[vmem, pl.BlockSpec(memory_space=pltpu.SMEM), vmem, vmem, vmem],
+        out_specs=(vmem, vmem),
+        compiler_params=pltpu.CompilerParams(vmem_limit_bytes=4 * 2**20),
+        cost_estimate=pl.CostEstimate(flops=10**10, bytes_accessed=2**20, transcendentals=0),
+        name="ask",
+    )(begun, lengths, queries, new_kv[:, 0, :], page_table)
     asked = lax.all_to_all(asked, "dp", 0, 0).reshape(requests, q_width + 2 * list_len)
 
     parts = pl.pallas_call(
         functools.partial(attend_kernel, scaling, n_dp),
         out_shape=jax.ShapeDtypeStruct((requests * heads, width), BF16),
-        in_specs=[pl.BlockSpec(memory_space=pltpu.VMEM)] * 2,
-        out_specs=pl.BlockSpec(memory_space=pltpu.VMEM),
+        in_specs=[vmem, vmem],
+        out_specs=vmem,
         scratch_shapes=[
             pltpu.VMEM((pool_home * heads, page_len), F32),
             pltpu.VMEM((pool_home * heads, head_dim), F32),
         ],
-        compiler_params=pltpu.CompilerParams(vmem_limit_bytes=16 * 2**20),
+        compiler_params=pltpu.CompilerParams(vmem_limit_bytes=12 * 2**20),
+        cost_estimate=pl.CostEstimate(flops=10**10, bytes_accessed=2**22, transcendentals=0),
         name="attend",
     )(asked, kv_pages[0])
 
     parts = lax.all_to_all(parts.reshape(n_dp, req_home * heads, width), "dp", 0, 0)
 
     own = features // n_tensor
-    step = 2
     partial_out = pl.pallas_call(
-        functools.partial(project_kernel, scaling),
-        grid=(n_tensor // step,),
+        project_kernel,
         out_shape=jax.ShapeDtypeStruct((n_tensor, req_home, own), BF16),
-        in_specs=[
-            pl.BlockSpec(memory_space=pltpu.VMEM),
-            pl.BlockSpec(memory_space=pltpu.VMEM),
-            pl.BlockSpec(memory_space=pltpu.VMEM),
-            pl.BlockSpec((q_width, step * own), lambda i: (0, i)),
-        ],
-        out_specs=pl.BlockSpec((step, req_home, own), lambda i: (i, 0, 0)),
-        scratch_shapes=[pltpu.VMEM((req_home, q_width), BF16)],
-        compiler_params=pltpu.CompilerParams(vmem_limit_bytes=16 * 2**20),
+        in_specs=[vmem, vmem, vmem],
+        out_specs=vmem,
+        compiler_params=pltpu.CompilerParams(vmem_limit_bytes=24 * 2**20),
+        cost_estimate=pl.CostEstimate(flops=10**9, bytes_accessed=2**24, transcendentals=0),
         name="project",
-    )(parts, queries, new_kv[:, 0, :], out_weight)
+    )(parts, state, out_weight)
 
     pieces = lax.all_to_all(partial_out, "tensor", 0, 0)
     return jnp.sum(pieces.astype(F32), axis=0).astype(BF16)

time: 54.8 us -> 42 us (0.77)
  local copies, waits for them, and re-layouts: 10 us -> 0.75 us
  other arithmetic: 2.89 us -> 0.65 us
  Pallas kernels: 6.47 us -> 5.08 us
    unnamed x8 -> x18, local copies, waits for them, and re-layouts: 9.34 us -> 0.75 us
    convert_element_type x2 -> x0, other arithmetic: 1.49 us -> none  [the longest x1 0.77 us: body(): named = jnp.where(valid, inside.astype(F32), NO_PAGE).astype(BF16)]
    pallas_call x1 -> x3, Pallas kernels: 4.46 us -> 3.07 us  [the longest x1 2.44 us: body(): pl.pallas_call(project_kernel, out_shape=jax.ShapeDtypeStruct((n_tensor,...]
    gt x1 -> x0, other arithmetic: 0.73 us -> none  [body(): valid = (inside >= 0) & (inside < pool_home) & (filled > 0)[None]]
    broadcast_in_dim x2 -> x0, local copies, waits for them, and re-layouts: 0.71 us -> none  [the longest x1 0.7 us: body(): jnp.broadcast_to(queries[None], (n_dp, req_home, q_width))]
where the time goes in v2:
time: 42 us; the launch traced here: 41.8 us
  blocking collectives  35.2 us (84%)
  Pallas kernels  5.08 us (12%)
  local copies, waits for them, and re-layouts  0.75 us (2%)
  other arithmetic  0.65 us (2%)
    all_to_all x1, blocking collectives, body(): pieces = lax.all_to_all(partial_out, 'tensor', 0, 0)  16.2 us
    all_to_all x1, blocking collectives, body(): lax.all_to_all(asked, 'dp', 0, 0).reshape(requests, q_width + 2 * list_len)  10.4 us
    all_to_all x1, blocking collectives, body(): lax.all_to_all(parts.reshape(n_dp, req_home * heads, width), 'dp', 0, 0)  8.65 us
    pallas_call x1, Pallas kernels, body(): pl.pallas_call(project_kernel, out_shape=jax.ShapeDtypeStruct((n_tensor,...  2.44 us
    pallas_call x1, Pallas kernels, body(): pl.pallas_call(functools.partial(attend_kernel, scaling, n_dp), out_shape...  2.01 us

profile of v2, /device:TPU:0, one launch (start us, length us, event | category | flops | bytes accessed | tf_op | source)
XLA Modules:
  0.0 41.8 jit_solution(909886001382082904)
XLA Ops:
  0.0 0.0 copy-start.3
  0.0 0.0 copy-start.4
  0.0 0.0 copy-start.2
  0.0 0.0 copy-start.1
  0.0 0.7 %copy-done.3 = s32[8,128]{1,0:T(8,128)S(1)} copy-done((s32[8,128]{1,0:T(8,128)S(1)}, s32[8,128]{1,0:T(8,128)}, u32[]{:S(2)}) %copy-start.3) | copy-done | bytes 4120
  0.7 0.0 copy-done.4
  0.7 0.0 copy-done.2
  0.7 0.0 copy-done.1
  0.7 0.0 copy-start
  0.7 0.0 slice-start
  0.8 0.0 slice-start.1
  0.8 0.6 %ask.1 = (bf16[8,8,768]{2,1,0:T(8,128)(2,1)S(1)}, f32[32,256]{1,0:T(8,128)S(1)}) custom-call(s32[8,128]{1,0:T(8,128)S(1)} %begin.1._, s32[8]{0:T(128)S(1)} %copy-done.4, bf16[8,512]{1,0:T(8,128)(2,1)S(1)} %copy-done.1, bf16[8,256]{1,0:T(8,128)(2,1)S(1)} %bitcast.9, s32[8,128]{1,0:T(8,128)S(1)} %copy-done.3), custom_call_target="tpu_custom_call" | custom-call | flops 10000000000 | bytes 1048576 | tf_op jit(solution)/shard_map/ask/pallas_call | solution.py:211
  1.4 10.4 %all_to_all.15 = bf16[8,8,768]{2,1,0:T(8,128)(2,1)S(1)} all-to-all(bf16[8,8,768]{2,1,0:T(8,128)(2,1)S(1)} %get-tuple-element.7), channel_id=1, replica_groups=mesh['dp'=8,'tensor'=16] {'dp'}, dimensions={0} | all-to-all | bytes 196608 | tf_op jit(solution)/shard_map/all_to_all | solution.py:223
  11.8 0.0 copy-done
  11.8 0.0 slice-start.2
  11.8 0.0 slice-start.3
  11.8 2.0 %attend.1 = bf16[256,256]{1,0:T(8,128)(2,1)S(1)} custom-call(bf16[64,768]{1,0:T(8,128)(2,1)S(1)} %bitcast.7, bf16[64,128,256]{2,1,0:T(8,128)(2,1)S(1)} %bitcast.8), custom_call_target="tpu_custom_call" | custom-call | flops 10000000000 | bytes 4194304 | tf_op jit(solution)/shard_map/attend/pallas_call | solution.py:225
  13.8 8.7 %all_to_all.16.parts_ref = bf16[8,32,256]{2,1,0:T(8,128)(2,1)S(1)} all-to-all(bf16[8,32,256]{2,1,0:T(8,128)(2,1)S(1)} %bitcast.6), channel_id=1, replica_groups=mesh['dp'=8,'tensor'=16] {'dp'}, dimensions={0} | all-to-all | bytes 262144 | tf_op jit(solution)/shard_map/all_to_all | solution.py:239
  22.5 0.0 slice-done
  22.5 0.0 slice-done.1
  22.5 0.0 slice-done.2
  22.5 0.0 slice-done.3
  22.5 2.4 %project.1 = bf16[16,8,1024]{2,1,0:T(8,128)(2,1)S(1)} custom-call(bf16[8,32,256]{2,1,0:T(8,128)(2,1)S(1)} %all_to_all.16.parts_ref, f32[32,256]{1,0:T(8,128)S(1)} %get-tuple-element.8.state_ref, bf16[512,16384]{1,0:T(8,128)(2,1)S(1)} %bitcast.5), custom_call_target="tpu_custom_call" | custom-call | flops 1000000000 | bytes 16777216 | tf_op jit(solution)/shard_map/project/pallas_call | solution.py:242
  24.9 16.2 %all_to_all.17 = bf16[16,8,1024]{2,1,0:T(8,128)(2,1)S(1)} all-to-all(bf16[16,8,1024]{2,1,0:T(8,128)(2,1)S(1)} %project.1), channel_id=1, replica_groups=mesh['dp'=8,'tensor'=16] {'tensor'}, dimensions={0} | all-to-all | bytes 524288 | tf_op jit(solution)/shard_map/all_to_all | solution.py:252
  41.1 0.6 %reduce_sum.12 = bf16[8,1024]{1,0:T(8,128)(2,1)} reduce(bf16[16,8,1024]{2,1,0:T(8,128)(2,1)S(1)} %all_to_all.17, bf16[]{:T(256)} %constant.2.clone.1), dimensions={0}, to_apply=%region_0.0 | reduce | flops 122880 | bytes 278530 | tf_op jit(solution)/shard_map/reduce_sum | solution.py:253
  (2 shorter events, 0.0 us)
Async XLA Ops:
  0.0 0.7 %copy-start.3 = (s32[8,128]{1,0:T(8,128)S(1)}, s32[8,128]{1,0:T(8,128)}, u32[]{:S(2)}) copy-start(s32[8,128]{1,0:T(8,128)} %table_ref.1) | copy-start | bytes 12292
  0.0 0.7 %copy-start.4 = (s32[8]{0:T(128)S(1)}, s32[8]{0:T(128)}, u32[]{:S(2)}) copy-start(s32[8]{0:T(128)} %length_ref.1) | copy-start | bytes 100
  0.0 0.7 %copy-start.2 = (bf16[8,1,256]{2,0,1:T(8,128)(2,1)S(1)}, bf16[8,1,256]{2,0,1:T(8,128)(2,1)}, u32[]{:S(2)}) copy-start(bf16[8,1,256]{2,0,1:T(8,128)(2,1)} %param.7) | copy-start | bytes 12292
  0.0 0.7 %copy-start.1 = (bf16[8,512]{1,0:T(8,128)(2,1)S(1)}, bf16[8,512]{1,0:T(8,128)(2,1)}, u32[]{:S(2)}) copy-start(bf16[8,512]{1,0:T(8,128)(2,1)} %query_ref.1) | copy-start | bytes 24580
  0.7 11.0 %copy-start = (bf16[1,64,128,256]{3,2,1,0:T(8,128)(2,1)S(1)}, bf16[1,64,128,256]{3,2,1,0:T(8,128)(2,1)}, u32[]{:S(2)}) copy-start(bf16[1,64,128,256]{3,2,1,0:T(8,128)(2,1)} %param.8) | copy-start | bytes 12582916
  0.7 21.7 %slice-start = ((s8[16777216]{0:T(1024)(128)(4,1)}), s8[4194304]{0:T(1024)(128)(4,1)S(1)}, s32[]{:S(2)}) async-start(s8[16777216]{0:T(1024)(128)(4,1)} %bitcast.4), calls=%async_computation.3 | async-start | bytes 8388608
  0.8 21.7 %slice-start.1 = ((s8[16777216]{0:T(1024)(128)(4,1)}), s8[4194304]{0:T(1024)(128)(4,1)S(1)}, s32[]{:S(2)}) async-start(s8[16777216]{0:T(1024)(128)(4,1)} %bitcast.4), calls=%async_computation.4 | async-start | bytes 8388608
  11.8 10.7 %slice-start.2 = ((s8[16777216]{0:T(1024)(128)(4,1)}), s8[4194304]{0:T(1024)(128)(4,1)S(1)}, s32[]{:S(2)}) async-start(s8[16777216]{0:T(1024)(128)(4,1)} %bitcast.4), calls=%async_computation.5 | async-start | bytes 8388608
  11.8 10.7 %slice-start.3 = ((s8[16777216]{0:T(1024)(128)(4,1)}), s8[4194304]{0:T(1024)(128)(4,1)S(1)}, s32[]{:S(2)}) async-start(s8[16777216]{0:T(1024)(128)(4,1)} %bitcast.4), calls=%async_computation.6 | async-start | bytes 8388608

commit v3 on v2

v3 whole, which is shorter than its diff:
```python
import functools

import jax
import jax.numpy as jnp
from jax import lax
from jax.experimental import pallas as pl
from jax.experimental.pallas import tpu as pltpu
from jax.sharding import PartitionSpec as P

FAR_BELOW = -1e30
LANES = 128
F32 = jnp.float32
BF16 = jnp.bfloat16
PAGE_SHIFT = 256
NO_PAGE = 1024.0
CORES = 2
GROUP = 8


def iota(shape, axis):
    return lax.broadcasted_iota(jnp.int32, shape, axis)


def begin_kernel(out_ref):
    out_ref[...] = jnp.zeros_like(out_ref)


def ask_kernel(
    scaling, page_len, _, length_ref, query_ref, newest_ref, table_ref, asked_ref, state_ref
):
    req, q_width = query_ref.shape
    list_len = table_ref.shape[1]
    head_dim = newest_ref.shape[1] // 2
    heads = q_width // head_dim
    length = jnp.broadcast_to(length_ref[...], (req, req))
    length = jnp.where(iota((req, req), 0) == iota((req, req), 1), length, 0).astype(F32)
    length = jnp.sum(length, axis=1, keepdims=True)
    first = (iota((req, list_len), 1) * page_len).astype(F32)
    query = query_ref[...]
    asked_ref[:, :q_width] = query
    asked_ref[:, q_width : q_width + list_len] = (
        (table_ref[...] - PAGE_SHIFT).astype(F32).astype(BF16)
    )
    asked_ref[:, q_width + list_len :] = jnp.clip(length - first, 0.0, float(page_len)).astype(BF16)
    newest = newest_ref[...].astype(F32)
    wide = query.astype(F32)
    fresh = jnp.zeros((req, LANES), F32)
    for h in range(heads):
        product = wide[:, h * head_dim : (h + 1) * head_dim] * newest[:, :head_dim]
        score = jnp.sum(product, axis=1, keepdims=True) * scaling
        fresh = jnp.where(iota((req, LANES), 1) == h, score, fresh)
    state_ref[:, :head_dim] = newest[:, head_dim:]
    state_ref[:, head_dim:] = fresh


def attend_kernel(scaling, heads, chip_ref, *refs):
    *other_refs, kv_ref, out_ref = refs
    asked_refs = (chip_ref, *other_refs)
    pages, page_len, width = kv_ref.shape
    head_dim = width // 2
    per_chip = chip_ref.shape[0]
    requests = per_chip * len(asked_refs)
    per_home = per_chip // CORES
    q_width = heads * head_dim

    page_id = iota((pages, LANES), 0).astype(F32) + (
        lax.axis_index("dp") * pages - PAGE_SHIFT
    ).astype(F32)
    found = jnp.zeros((pages, LANES), F32)
    for k, asked_ref in enumerate(asked_refs):
        filled = asked_ref[:, q_width + LANES : q_width + 2 * LANES].astype(F32)
        named = asked_ref[:, q_width : q_width + LANES].astype(F32)
        named = jnp.where(filled > 0.0, named, NO_PAGE)
        coded = filled + (iota(filled.shape, 0) + k * per_chip).astype(F32) * 256.0
        for r in range(per_chip):
            found = jnp.where(named[r : r + 1, :] == page_id, coded[r : r + 1, :], found)
    code = jnp.broadcast_to(jnp.sum(found, axis=1, keepdims=True), (pages, LANES))
    owner = jnp.floor(code * (1.0 / 256.0))
    alive = iota((pages, page_len), 1).astype(F32) < code - owner * 256.0
    owns = owner == iota((pages, LANES), 1).astype(F32)
    picker = jnp.where(owns, 1.0, 0.0)

    asked = jnp.concatenate([ref[:, :q_width] for ref in asked_refs], axis=0)
    picked = jnp.dot(picker[:, :requests].astype(BF16), asked, preferred_element_type=F32)
    query = [picked[:, h * head_dim : (h + 1) * head_dim] for h in range(heads)]

    member = iota((GROUP, LANES), 0)
    scores = [[] for _ in range(heads)]
    for j in range(pages // GROUP):
        here = slice(j * GROUP, (j + 1) * GROUP)
        keys = kv_ref[here, :, :head_dim].reshape(GROUP * page_len, head_dim)
        full = lax.dot_general(
            jnp.concatenate([query[h][here] for h in range(heads)], axis=0).astype(BF16),
            keys,
            (((1,), (1,)), ((), ())),
            preferred_element_type=F32,
        )
        for h in range(heads):
            rows = full[h * GROUP : (h + 1) * GROUP]
            mine = rows[:, :page_len]
            for g in range(1, GROUP):
                mine = jnp.where(member == g, rows[:, g * page_len : (g + 1) * page_len], mine)
            scores[h].append(mine)
    page_peak, page_total, local = [], [], []
    for h in range(heads):
        score = jnp.where(alive, jnp.concatenate(scores[h], axis=0) * scaling, FAR_BELOW)
        page_peak.append(jnp.max(score, axis=1, keepdims=True))
        local.append(jnp.where(alive, jnp.exp(score - page_peak[h]), 0.0))
        page_total.append(jnp.sum(local[h], axis=1, keepdims=True))
    values = [[] for _ in range(heads)]
    for j in range(pages // GROUP):
        here = slice(j * GROUP, (j + 1) * GROUP)
        weights = jnp.concatenate(
            [
                jnp.concatenate(
                    [jnp.where(member == g, local[h][here], 0.0) for g in range(GROUP)], axis=1
                )
                for h in range(heads)
            ],
            axis=0,
        ).astype(BF16)
        group_values = jnp.dot(
            weights,
            kv_ref[here, :, head_dim:].reshape(GROUP * page_len, head_dim),
            preferred_element_type=F32,
        )
        for h in range(heads):
            values[h].append(group_values[h * GROUP : (h + 1) * GROUP])

    points, totals, scaled = [], [], []
    for h in range(heads):
        peak = jnp.max(jnp.where(owns, page_peak[h], FAR_BELOW), axis=0, keepdims=True)
        point = peak.astype(BF16).astype(F32)
        shift = jnp.max(jnp.where(owns, point, FAR_BELOW), axis=1, keepdims=True)
        factor = jnp.exp(jnp.minimum(page_peak[h] - shift, 80.0))
        total = jnp.sum(jnp.where(owns, page_total[h] * factor, 0.0), axis=0, keepdims=True)
        points.append(point)
        totals.append(total)
        scaled.append(jnp.concatenate(values[h], axis=0) * factor)
    scaled = jnp.concatenate(scaled, axis=1)
    high = scaled.astype(BF16)
    low = (scaled - high.astype(F32)).astype(BF16)
    chosen = picker.T[:requests].astype(BF16)
    summed = jnp.dot(chosen, high, preferred_element_type=F32) + jnp.dot(
        chosen, low, preferred_element_type=F32
    )
    summed = summed.astype(BF16)
    high = [total.astype(BF16).astype(F32) for total in totals]
    low = [total - part for total, part in zip(totals, high)]
    points = jnp.concatenate(points + points, axis=0).T
    totals = jnp.concatenate(high + low, axis=0).T
    wide = jnp.zeros((requests, LANES - 2 * heads), F32)
    points = jnp.concatenate([points[:requests], wide], axis=1)
    totals = jnp.concatenate([totals[:requests], wide], axis=1)
    for g in range(requests // per_home):
        home = lax.axis_index("dp") ^ g
        here = slice(g * per_home, (g + 1) * per_home)
        block = [summed[here, h * head_dim : (h + 1) * head_dim] for h in range(heads)]
        out_ref[home] = jnp.concatenate(
            block + [points[here].astype(BF16), totals[here].astype(BF16)], axis=0
        )


def project_kernel(part_ref, state_ref, weight_ref, out_ref):
    sources, rows, head_dim = part_ref.shape
    blocks, req, own = out_ref.shape
    heads = rows // req - 2
    fresh = state_ref[:, head_dim:]
    points = [part_ref[s, heads * req :, :].astype(F32)[:req] for s in range(sources)]
    peak = fresh
    for point in points:
        peak = jnp.maximum(peak, point)
    weight = jnp.exp(fresh - peak)
    total = weight
    summed = [weight[:, h : h + 1] * state_ref[:, :head_dim] for h in range(heads)]
    for s in range(sources):
        factor = jnp.exp(points[s] - peak)
        addends = part_ref[s, heads * req :, :].astype(F32)[req:]
        total = total + factor * (addends + pltpu.roll(addends, LANES - heads, 1))
        for h in range(heads):
            value = part_ref[s, h * req : (h + 1) * req, :].astype(F32)
            summed[h] = summed[h] + factor[:, h : h + 1] * value
    given = jnp.concatenate(
        [summed[h] / total[:, h : h + 1] for h in range(heads)], axis=1
    ).astype(BF16)
    for k in range(blocks):
        out_ref[k] = jnp.dot(
            given, weight_ref[:, k * own : (k + 1) * own], preferred_element_type=F32
        ).astype(BF16)


def body(n_dp, n_tensor, queries, new_kv, kv_pages, lengths, page_table, out_weight):
    req_home, q_width = queries.shape
    _, pool_home, page_len, width = kv_pages.shape
    head_dim = width // 2
    heads = q_width // head_dim
    list_len = page_table.shape[1]
    features = out_weight.shape[1]
    requests = req_home * n_dp
    scaling = head_dim ** (-0.5)

    vmem = pl.BlockSpec(memory_space=pltpu.VMEM)
    def swap(x, mask):
        return lax.ppermute(x, "dp", [(i, i ^ mask) for i in range(n_dp)])

    begun = pl.pallas_call(
        begin_kernel,
        out_shape=jax.ShapeDtypeStruct((8, LANES), jnp.int32),
        out_specs=vmem,
        compiler_params=pltpu.CompilerParams(vmem_limit_bytes=2**20),
        cost_estimate=pl.CostEstimate(flops=10**10, bytes_accessed=2**20, transcendentals=0),
        name="begin",
    )()
    asked, state = pl.pallas_call(
        functools.partial(ask_kernel, scaling, page_len),
        out_shape=(
            jax.ShapeDtypeStruct((req_home, q_width + 2 * list_len), BF16),
            jax.ShapeDtypeStruct((req_home, width), F32),
        ),
        in_specs=[vmem] * 5,
        out_specs=(vmem, vmem),
        compiler_params=pltpu.CompilerParams(vmem_limit_bytes=4 * 2**20),
        cost_estimate=pl.CostEstimate(flops=10**10, bytes_accessed=2**20, transcendentals=0),
        name="ask",
    )(begun, lengths.reshape(1, req_home), queries, new_kv[:, 0, :], page_table)
    asked = jnp.concatenate([asked, swap(asked, 1)], axis=0)
    chips = n_dp // CORES
    others = [swap(asked, CORES * k) for k in range(1, chips)]
    parts = pl.pallas_call(
        functools.partial(attend_kernel, scaling, heads),
        out_shape=jax.ShapeDtypeStruct((n_dp, req_home * (heads + 2), head_dim), BF16),
        in_specs=[vmem] * (chips + 1),
        out_specs=vmem,
        compiler_params=pltpu.CompilerParams(vmem_limit_bytes=12 * 2**20),
        cost_estimate=pl.CostEstimate(flops=10**10, bytes_accessed=2**22, transcendentals=0),
        name="attend",
    )(asked, *others, kv_pages[0])
    parts = lax.all_to_all(parts, "dp", 0, 0)

    own = features // n_tensor
    partial_out = pl.pallas_call(
        project_kernel,
        out_shape=jax.ShapeDtypeStruct((n_tensor, req_home, own), BF16),
        in_specs=[vmem] * 3,
        out_specs=vmem,
        compiler_params=pltpu.CompilerParams(vmem_limit_bytes=24 * 2**20),
        cost_estimate=pl.CostEstimate(flops=10**9, bytes_accessed=2**24, transcendentals=0),
        name="project",
    )(parts, state, out_weight)

    pieces = lax.all_to_all(partial_out, "tensor", 0, 0)
    return jnp.sum(pieces.astype(F32), axis=0).astype(BF16)


def solution(mesh):
    return jax.shard_map(
        functools.partial(body, mesh.shape["dp"], mesh.shape["tensor"]),
        mesh=mesh,
        in_specs=(
            P("dp", "tensor"),
            P("dp", "tensor", None),
            P("tensor", "dp", None, None),
            P("dp"),
            P("dp", None),
            P("tensor", None),
        ),
        out_specs=P("dp", "tensor"),
        check_vma=False,
    )
```

time: 42 us -> 40.7 us (0.969)
  blocking collectives: 35.2 us -> 25.3 us
  waiting for transfers between devices: 0 us -> 5.49 us
  starting transfers between devices: 0 us -> 4.11 us
  Pallas kernels: 5.08 us -> 4.04 us
    all_to_all x2 -> x1, blocking collectives: 19.1 us -> 9.15 us  [body(): parts = lax.all_to_all(parts, 'dp', 0, 0)]
    ppermute x0 -> x4, waiting for transfers between devices: none -> 5.49 us  [swap(): return lax.ppermute(x, 'dp', [(i, i ^ mask) for i in range(n_dp)])]
    ppermute x0 -> x4, starting transfers between devices: none -> 4.11 us  [swap(): return lax.ppermute(x, 'dp', [(i, i ^ mask) for i in range(n_dp)])]
    pallas_call x2, Pallas kernels: 2.63 us -> 1.62 us  [the longest x1 1.54 us: body(): pl.pallas_call(functools.partial(attend_kernel, scaling, heads), out_shap...]
  transfers between devices with their start and end apart: 0 -> 4, of which waited for: 0 -> 3; matrix products, arithmetic and copies ran while one was open for 0% -> 0% of each run, Pallas kernels for 0% -> 0%
where the time goes in v3:
time: 40.7 us; the launch traced here: 40.5 us
  blocking collectives  25.3 us (62%)
  waiting for transfers between devices  5.49 us (13%)
  starting transfers between devices  4.11 us (10%)
  Pallas kernels  4.04 us (10%)
  local copies, waits for them, and re-layouts  0.76 us (2%)
  other arithmetic  0.65 us (2%)
    all_to_all x1, blocking collectives, body(): pieces = lax.all_to_all(partial_out, 'tensor', 0, 0)  16.2 us
    all_to_all x1, blocking collectives, body(): parts = lax.all_to_all(parts, 'dp', 0, 0)  9.15 us
    ppermute x4, waiting for transfers between devices, swap(): return lax.ppermute(x, 'dp', [(i, i ^ mask) for i in range(n_dp)])  5.49 us
    ppermute x4, starting transfers between devices, swap(): return lax.ppermute(x, 'dp', [(i, i ^ mask) for i in range(n_dp)])  4.11 us
    pallas_call x1, Pallas kernels, body(): pl.pallas_call(project_kernel, out_shape=jax.ShapeDtypeStruct((n_tensor,...  2.42 us
    pallas_call x1, Pallas kernels, body(): pl.pallas_call(functools.partial(attend_kernel, scaling, heads), out_shap...  1.54 us
  transfers between devices with their start and end apart: 4, of which 3 were waited for; matrix products, arithmetic and copies ran while one was open for 0% of the time, Pallas kernels for 0%

profile of v3, /device:TPU:0, one launch (start us, length us, event | category | flops | bytes accessed | tf_op | source)
XLA Modules:
  0.0 40.5 jit_solution(2610936456975116772)
XLA Ops:
  0.0 0.0 copy-start.3
  0.0 0.0 copy-start.4
  0.0 0.0 copy-start.2
  0.0 0.0 copy-start.1
  0.0 0.7 %copy-done.3 = s32[8,128]{1,0:T(8,128)S(1)} copy-done((s32[8,128]{1,0:T(8,128)S(1)}, s32[8,128]{1,0:T(8,128)}, u32[]{:S(2)}) %copy-start.3) | copy-done | bytes 4120
  0.7 0.0 copy-done.4
  0.7 0.0 copy-done.2
  0.7 0.0 copy-done.1
  0.7 0.0 copy-start
  0.7 0.0 slice-start
  0.8 0.0 slice-start.1
  0.8 0.1 ask.1
  0.8 0.0 collective-permute-start
  0.9 1.2 %collective-permute-done = bf16[8,768]{1,0:T(8,128)(2,1)S(1)} collective-permute-done((bf16[8,768]{1,0:T(8,128)(2,1)S(1)}, bf16[8,768]{1,0:T(8,128)(2,1)S(1)}, u32[]{:S(2)}, u32[]{:S(2)}) %collective-permute-start) | collective-permute-done | bytes 12320 | tf_op jit(solution)/shard_map/ppermute | solution.py:204
  2.0 3.1 %collective-permute-start.3 = (bf16[16,768]{1,0:T(8,128)(2,1)S(1)}, bf16[16,768]{1,0:T(8,128)(2,1)S(1)}, u32[]{:S(2)}, u32[]{:S(2)}) collective-permute-start(bf16[16,768]{1,0:T(8,128)(2,1)S(1)} %constant_dynamic-update-slice_fusion.chip_ref), channel_id=1, source_target_pairs={{0,96},{16,112},{32,64},{48,80},{64,32},{80,48},{96,0},{112,16},{1... | collective-permute-start | bytes 73736 | tf_op jit(solution)/shard_map/ppermute | solution.py:204
  5.1 0.6 %collective-permute-start.2 = (bf16[16,768]{1,0:T(8,128)(2,1)S(1)}, bf16[16,768]{1,0:T(8,128)(2,1)S(1)}, u32[]{:S(2)}, u32[]{:S(2)}) collective-permute-start(bf16[16,768]{1,0:T(8,128)(2,1)S(1)} %constant_dynamic-update-slice_fusion.chip_ref), channel_id=1, source_target_pairs={{0,64},{16,80},{32,96},{48,112},{64,0},{80,16},{96,32},{112,48},{1... | collective-permute-start | bytes 73736 | tf_op jit(solution)/shard_map/ppermute | solution.py:204
  5.8 0.4 collective-permute-start.1
  6.1 0.9 %collective-permute-done.3.refs_2_ = bf16[16,768]{1,0:T(8,128)(2,1)S(1)} collective-permute-done((bf16[16,768]{1,0:T(8,128)(2,1)S(1)}, bf16[16,768]{1,0:T(8,128)(2,1)S(1)}, u32[]{:S(2)}, u32[]{:S(2)}) %collective-permute-start.3) | collective-permute-done | bytes 24608 | tf_op jit(solution)/shard_map/ppermute | solution.py:204
  7.1 3.4 %collective-permute-done.2.refs_1_ = bf16[16,768]{1,0:T(8,128)(2,1)S(1)} collective-permute-done((bf16[16,768]{1,0:T(8,128)(2,1)S(1)}, bf16[16,768]{1,0:T(8,128)(2,1)S(1)}, u32[]{:S(2)}, u32[]{:S(2)}) %collective-permute-start.2) | collective-permute-done | bytes 24608 | tf_op jit(solution)/shard_map/ppermute | solution.py:204
  10.5 0.0 collective-permute-done.1.refs_0_
  10.5 0.0 copy-done
  10.5 0.0 slice-start.2
  10.5 0.0 slice-start.3
  10.5 1.5 %attend.1 = bf16[8,48,128]{2,1,0:T(8,128)(2,1)S(1)} custom-call(bf16[16,768]{1,0:T(8,128)(2,1)S(1)} %constant_dynamic-update-slice_fusion.chip_ref, bf16[16,768]{1,0:T(8,128)(2,1)S(1)} %collective-permute-done.1.refs_0_, bf16[16,768]{1,0:T(8,128)(2,1)S(1)} %collective-permute-done.2.refs_1_, bf16[16,768]{1,0:T(8,128)(2,1)S(1)} %collective-permute-done.3.refs_2_, ...), custom_call_target="tpu_custom_call" | custom-call | flops 10000000000 | bytes 4194304 | tf_op jit(solution)/shard_map/attend/pallas_call | solution.py:229
  12.0 9.1 %all_to_all.10.part_ref = bf16[8,48,128]{2,1,0:T(8,128)(2,1)S(1)} all-to-all(bf16[8,48,128]{2,1,0:T(8,128)(2,1)S(1)} %attend.1), channel_id=1, replica_groups=mesh['dp'=8,'tensor'=16] {'dp'}, dimensions={0} | all-to-all | bytes 196608 | tf_op jit(solution)/shard_map/all_to_all | solution.py:238
  21.2 0.0 slice-done
  21.2 0.0 slice-done.1
  21.2 0.0 slice-done.2
  21.2 0.0 slice-done.3
  21.2 2.4 %project.1 = bf16[16,8,1024]{2,1,0:T(8,128)(2,1)S(1)} custom-call(bf16[8,48,128]{2,1,0:T(8,128)(2,1)S(1)} %all_to_all.10.part_ref, f32[8,256]{1,0:T(8,128)S(1)} %get-tuple-element.8.state_ref, bf16[512,16384]{1,0:T(8,128)(2,1)S(1)} %bitcast.4), custom_call_target="tpu_custom_call" | custom-call | flops 1000000000 | bytes 16777216 | tf_op jit(solution)/shard_map/project/pallas_call | solution.py:241
  23.6 16.2 %all_to_all.11 = bf16[16,8,1024]{2,1,0:T(8,128)(2,1)S(1)} all-to-all(bf16[16,8,1024]{2,1,0:T(8,128)(2,1)S(1)} %project.1), channel_id=1, replica_groups=mesh['dp'=8,'tensor'=16] {'tensor'}, dimensions={0} | all-to-all | bytes 524288 | tf_op jit(solution)/shard_map/all_to_all | solution.py:251
  39.8 0.6 %reduce_sum.12 = bf16[8,1024]{1,0:T(8,128)(2,1)} reduce(bf16[16,8,1024]{2,1,0:T(8,128)(2,1)S(1)} %all_to_all.11, bf16[]{:T(256)} %constant.2.clone.1), dimensions={0}, to_apply=%region_0.0 | reduce | flops 122880 | bytes 278530 | tf_op jit(solution)/shard_map/reduce_sum | solution.py:252
  (4 shorter events, 0.0 us)
Async XLA Ops:
  0.0 0.7 %copy-start.3 = (s32[8,128]{1,0:T(8,128)S(1)}, s32[8,128]{1,0:T(8,128)}, u32[]{:S(2)}) copy-start(s32[8,128]{1,0:T(8,128)} %table_ref.1) | copy-start | bytes 12292
  0.0 0.7 %copy-start.4 = (s32[8]{0:T(128)S(1)}, s32[8]{0:T(128)}, u32[]{:S(2)}) copy-start(s32[8]{0:T(128)} %param.9) | copy-start | bytes 100
  0.0 0.7 %copy-start.2 = (bf16[8,1,256]{2,0,1:T(8,128)(2,1)S(1)}, bf16[8,1,256]{2,0,1:T(8,128)(2,1)}, u32[]{:S(2)}) copy-start(bf16[8,1,256]{2,0,1:T(8,128)(2,1)} %param.7) | copy-start | bytes 12292
  0.0 0.7 %copy-start.1 = (bf16[8,512]{1,0:T(8,128)(2,1)S(1)}, bf16[8,512]{1,0:T(8,128)(2,1)}, u32[]{:S(2)}) copy-start(bf16[8,512]{1,0:T(8,128)(2,1)} %query_ref.1) | copy-start | bytes 24580
  0.7 9.7 %copy-start = (bf16[1,64,128,256]{3,2,1,0:T(8,128)(2,1)S(1)}, bf16[1,64,128,256]{3,2,1,0:T(8,128)(2,1)}, u32[]{:S(2)}) copy-start(bf16[1,64,128,256]{3,2,1,0:T(8,128)(2,1)} %param.8) | copy-start | bytes 12582916
  0.7 20.4 %slice-start = ((s8[16777216]{0:T(1024)(128)(4,1)}), s8[4194304]{0:T(1024)(128)(4,1)S(1)}, s32[]{:S(2)}) async-start(s8[16777216]{0:T(1024)(128)(4,1)} %bitcast.3), calls=%async_computation.2 | async-start | bytes 8388608
  0.8 20.4 %slice-start.1 = ((s8[16777216]{0:T(1024)(128)(4,1)}), s8[4194304]{0:T(1024)(128)(4,1)S(1)}, s32[]{:S(2)}) async-start(s8[16777216]{0:T(1024)(128)(4,1)} %bitcast.3), calls=%async_computation.3 | async-start | bytes 8388608
  0.8 1.2 %collective-permute-start = (bf16[8,768]{1,0:T(8,128)(2,1)S(1)}, bf16[8,768]{1,0:T(8,128)(2,1)S(1)}, u32[]{:S(2)}, u32[]{:S(2)}) collective-permute-start(bf16[8,768]{1,0:T(8,128)(2,1)S(1)} %get-tuple-element.7), channel_id=1, source_target_pairs={{0,16},{16,0},{32,48},{48,32},{64,80},{80,64},{96,112},{112,96},{1... | collective-permute-start | bytes 36872 | tf_op jit(solution)/shard_map/ppermute | solution.py:204
  2.0 5.0 %collective-permute-start.3 = (bf16[16,768]{1,0:T(8,128)(2,1)S(1)}, bf16[16,768]{1,0:T(8,128)(2,1)S(1)}, u32[]{:S(2)}, u32[]{:S(2)}) collective-permute-start(bf16[16,768]{1,0:T(8,128)(2,1)S(1)} %constant_dynamic-update-slice_fusion.chip_ref), channel_id=1, source_target_pairs={{0,96},{16,112},{32,64},{48,80},{64,32},{80,48},{96,0},{112,16},{1... | collective-permute-start | bytes 73736 | tf_op jit(solution)/shard_map/ppermute | solution.py:204
  5.1 5.3 %collective-permute-start.2 = (bf16[16,768]{1,0:T(8,128)(2,1)S(1)}, bf16[16,768]{1,0:T(8,128)(2,1)S(1)}, u32[]{:S(2)}, u32[]{:S(2)}) collective-permute-start(bf16[16,768]{1,0:T(8,128)(2,1)S(1)} %constant_dynamic-update-slice_fusion.chip_ref), channel_id=1, source_target_pairs={{0,64},{16,80},{32,96},{48,112},{64,0},{80,16},{96,32},{112,48},{1... | collective-permute-start | bytes 73736 | tf_op jit(solution)/shard_map/ppermute | solution.py:204
  5.8 4.7 %collective-permute-start.1 = (bf16[16,768]{1,0:T(8,128)(2,1)S(1)}, bf16[16,768]{1,0:T(8,128)(2,1)S(1)}, u32[]{:S(2)}, u32[]{:S(2)}) collective-permute-start(bf16[16,768]{1,0:T(8,128)(2,1)S(1)} %constant_dynamic-update-slice_fusion.chip_ref), channel_id=1, source_target_pairs={{0,32},{16,48},{32,0},{48,16},{64,96},{80,112},{96,64},{112,80},{1... | collective-permute-start | bytes 73736 | tf_op jit(solution)/shard_map/ppermute | solution.py:204
  10.5 10.7 %slice-start.2 = ((s8[16777216]{0:T(1024)(128)(4,1)}), s8[4194304]{0:T(1024)(128)(4,1)S(1)}, s32[]{:S(2)}) async-start(s8[16777216]{0:T(1024)(128)(4,1)} %bitcast.3), calls=%async_computation.4 | async-start | bytes 8388608
  10.5 10.7 %slice-start.3 = ((s8[16777216]{0:T(1024)(128)(4,1)}), s8[4194304]{0:T(1024)(128)(4,1)S(1)}, s32[]{:S(2)}) async-start(s8[16777216]{0:T(1024)(128)(4,1)} %bitcast.3), calls=%async_computation.5 | async-start | bytes 8388608

commit v4 on v3

--- a/solution.py
+++ b/solution.py
@@ -37,11 +37,12 @@
     length = jnp.sum(length, axis=1, keepdims=True)
     first = (iota((req, list_len), 1) * page_len).astype(F32)
     query = query_ref[...]
-    asked_ref[:, :q_width] = query
-    asked_ref[:, q_width : q_width + list_len] = (
-        (table_ref[...] - PAGE_SHIFT).astype(F32).astype(BF16)
-    )
-    asked_ref[:, q_width + list_len :] = jnp.clip(length - first, 0.0, float(page_len)).astype(BF16)
+    named = (table_ref[...] - PAGE_SHIFT).astype(F32).astype(BF16)
+    filled = jnp.clip(length - first, 0.0, float(page_len)).astype(BF16)
+    for d in range(asked_ref.shape[0]):
+        asked_ref[d, :, :q_width] = query
+        asked_ref[d, :, q_width : q_width + list_len] = named
+        asked_ref[d, :, q_width + list_len :] = filled
     newest = newest_ref[...].astype(F32)
     wide = query.astype(F32)
     fresh = jnp.zeros((req, LANES), F32)
@@ -53,14 +54,14 @@
     state_ref[:, head_dim:] = fresh
 
 
-def attend_kernel(scaling, heads, chip_ref, *refs):
+def attend_kernel(scaling, homes, heads, chip_ref, *refs):
     *other_refs, kv_ref, out_ref = refs
     asked_refs = (chip_ref, *other_refs)
     pages, page_len, width = kv_ref.shape
     head_dim = width // 2
     per_chip = chip_ref.shape[0]
     requests = per_chip * len(asked_refs)
-    per_home = per_chip // CORES
+    per_home = requests // homes
     q_width = heads * head_dim
 
     page_id = iota((pages, LANES), 0).astype(F32) + (
@@ -153,10 +154,9 @@
     points = jnp.concatenate([points[:requests], wide], axis=1)
     totals = jnp.concatenate([totals[:requests], wide], axis=1)
     for g in range(requests // per_home):
-        home = lax.axis_index("dp") ^ g
         here = slice(g * per_home, (g + 1) * per_home)
         block = [summed[here, h * head_dim : (h + 1) * head_dim] for h in range(heads)]
-        out_ref[home] = jnp.concatenate(
+        out_ref[g] = jnp.concatenate(
             block + [points[here].astype(BF16), totals[here].astype(BF16)], axis=0
         )
 
@@ -200,9 +200,6 @@
     scaling = head_dim ** (-0.5)
 
     vmem = pl.BlockSpec(memory_space=pltpu.VMEM)
-    def swap(x, mask):
-        return lax.ppermute(x, "dp", [(i, i ^ mask) for i in range(n_dp)])
-
     begun = pl.pallas_call(
         begin_kernel,
         out_shape=jax.ShapeDtypeStruct((8, LANES), jnp.int32),
@@ -214,27 +211,25 @@
     asked, state = pl.pallas_call(
         functools.partial(ask_kernel, scaling, page_len),
         out_shape=(
-            jax.ShapeDtypeStruct((req_home, q_width + 2 * list_len), BF16),
+            jax.ShapeDtypeStruct((n_dp, req_home, q_width + 2 * list_len), BF16),
             jax.ShapeDtypeStruct((req_home, width), F32),
         ),
         in_specs=[vmem] * 5,
         out_specs=(vmem, vmem),
         compiler_params=pltpu.CompilerParams(vmem_limit_bytes=4 * 2**20),
-        cost_estimate=pl.CostEstimate(flops=10**10, bytes_accessed=2**20, transcendentals=0),
+        cost_estimate=pl.CostEstimate(flops=10**11, bytes_accessed=2**20, transcendentals=0),
         name="ask",
     )(begun, lengths.reshape(1, req_home), queries, new_kv[:, 0, :], page_table)
-    asked = jnp.concatenate([asked, swap(asked, 1)], axis=0)
-    chips = n_dp // CORES
-    others = [swap(asked, CORES * k) for k in range(1, chips)]
+    asked = lax.all_to_all(asked, "dp", 0, 0).reshape(requests, q_width + 2 * list_len)
     parts = pl.pallas_call(
-        functools.partial(attend_kernel, scaling, heads),
+        functools.partial(attend_kernel, scaling, n_dp, heads),
         out_shape=jax.ShapeDtypeStruct((n_dp, req_home * (heads + 2), head_dim), BF16),
-        in_specs=[vmem] * (chips + 1),
+        in_specs=[vmem] * 2,
         out_specs=vmem,
         compiler_params=pltpu.CompilerParams(vmem_limit_bytes=12 * 2**20),
         cost_estimate=pl.CostEstimate(flops=10**10, bytes_accessed=2**22, transcendentals=0),
         name="attend",
-    )(asked, *others, kv_pages[0])
+    )(asked, kv_pages[0])
     parts = lax.all_to_all(parts, "dp", 0, 0)
 
     own = features // n_tensor

time: 40.7 us -> 40.5 us (level)
  blocking collectives: 25.3 us -> 34.8 us
  waiting for transfers between devices: 5.49 us -> 0 us
  starting transfers between devices: 4.11 us -> 0 us
    all_to_all x0 -> x1, blocking collectives: none -> 10.4 us  [body(): lax.all_to_all(asked, 'dp', 0, 0).reshape(requests, q_width + 2 * list_len)]
    ppermute x4 -> x0, waiting for transfers between devices: 5.49 us -> none  [swap(): return lax.ppermute(x, 'dp', [(i, i ^ mask) for i in range(n_dp)])]
    ppermute x4 -> x0, starting transfers between devices: 4.11 us -> none  [swap(): return lax.ppermute(x, 'dp', [(i, i ^ mask) for i in range(n_dp)])]
    all_to_all x1, blocking collectives: 9.15 us -> 8.18 us  [body(): parts = lax.all_to_all(parts, 'dp', 0, 0)]
  transfers between devices with their start and end apart: 4 -> 0, of which waited for: 3 -> 0; matrix products, arithmetic and copies ran while one was open for 0% -> 0% of each run, Pallas kernels for 0% -> 0%
where the time goes in v4:
time: 40.5 us; the launch traced here: 40.3 us
  blocking collectives  34.8 us (86%)
  Pallas kernels  4.04 us (10%)
  local copies, waits for them, and re-layouts  0.74 us (2%)
  other arithmetic  0.65 us (2%)
    all_to_all x1, blocking collectives, body(): pieces = lax.all_to_all(partial_out, 'tensor', 0, 0)  16.2 us
    all_to_all x1, blocking collectives, body(): lax.all_to_all(asked, 'dp', 0, 0).reshape(requests, q_width + 2 * list_len)  10.4 us
    all_to_all x1, blocking collectives, body(): parts = lax.all_to_all(parts, 'dp', 0, 0)  8.18 us
    pallas_call x1, Pallas kernels, body(): pl.pallas_call(project_kernel, out_shape=jax.ShapeDtypeStruct((n_tensor,...  2.42 us
    pallas_call x1, Pallas kernels, body(): pl.pallas_call(functools.partial(attend_kernel, scaling, n_dp, heads), ou...  1.53 us

profile of v4, /device:TPU:0, one launch (start us, length us, event | category | flops | bytes accessed | tf_op | source)
XLA Modules:
  0.0 40.3 jit_solution(1713706806516848783)
XLA Ops:
  0.0 0.0 copy-start.3
  0.0 0.0 copy-start.4
  0.0 0.0 copy-start.2
  0.0 0.0 copy-start.1
  0.0 0.0 slice-start
  0.0 0.7 %copy-done.3 = s32[8,128]{1,0:T(8,128)S(1)} copy-done((s32[8,128]{1,0:T(8,128)S(1)}, s32[8,128]{1,0:T(8,128)}, u32[]{:S(2)}) %copy-start.3) | copy-done | bytes 4120
  0.7 0.0 copy-done.4
  0.7 0.0 copy-done.2
  0.7 0.0 copy-done.1
  0.7 0.0 copy-start
  0.7 0.0 slice-start.1
  0.8 0.0 slice-start.2
  0.8 0.0 slice-start.3
  0.8 0.1 ask.1
  0.8 10.4 %all_to_all.15 = bf16[8,8,768]{2,1,0:T(8,128)(2,1)S(1)} all-to-all(bf16[8,8,768]{2,1,0:T(8,128)(2,1)S(1)} %get-tuple-element.7), channel_id=1, replica_groups=mesh['dp'=8,'tensor'=16] {'dp'}, dimensions={0} | all-to-all | bytes 196608 | tf_op jit(solution)/shard_map/all_to_all | solution.py:223
  11.2 0.0 copy-done
  11.2 1.5 %attend.1 = bf16[8,48,128]{2,1,0:T(8,128)(2,1)S(1)} custom-call(bf16[64,768]{1,0:T(8,128)(2,1)S(1)} %bitcast.6, bf16[64,128,256]{2,1,0:T(8,128)(2,1)S(1)} %bitcast.7), custom_call_target="tpu_custom_call" | custom-call | flops 10000000000 | bytes 4194304 | tf_op jit(solution)/shard_map/attend/pallas_call | solution.py:224
  12.8 8.2 %all_to_all.16.part_ref = bf16[8,48,128]{2,1,0:T(8,128)(2,1)S(1)} all-to-all(bf16[8,48,128]{2,1,0:T(8,128)(2,1)S(1)} %attend.1), channel_id=1, replica_groups=mesh['dp'=8,'tensor'=16] {'dp'}, dimensions={0} | all-to-all | bytes 196608 | tf_op jit(solution)/shard_map/all_to_all | solution.py:233
  21.0 0.0 slice-done
  21.0 0.0 slice-done.1
  21.0 0.0 slice-done.2
  21.0 0.0 slice-done.3
  21.0 2.4 %project.1 = bf16[16,8,1024]{2,1,0:T(8,128)(2,1)S(1)} custom-call(bf16[8,48,128]{2,1,0:T(8,128)(2,1)S(1)} %all_to_all.16.part_ref, f32[8,256]{1,0:T(8,128)S(1)} %get-tuple-element.8.state_ref, bf16[512,16384]{1,0:T(8,128)(2,1)S(1)} %bitcast.5), custom_call_target="tpu_custom_call" | custom-call | flops 1000000000 | bytes 16777216 | tf_op jit(solution)/shard_map/project/pallas_call | solution.py:236
  23.4 16.2 %all_to_all.17 = bf16[16,8,1024]{2,1,0:T(8,128)(2,1)S(1)} all-to-all(bf16[16,8,1024]{2,1,0:T(8,128)(2,1)S(1)} %project.1), channel_id=1, replica_groups=mesh['dp'=8,'tensor'=16] {'tensor'}, dimensions={0} | all-to-all | bytes 524288 | tf_op jit(solution)/shard_map/all_to_all | solution.py:246
  39.6 0.6 %reduce_sum.12 = bf16[8,1024]{1,0:T(8,128)(2,1)} reduce(bf16[16,8,1024]{2,1,0:T(8,128)(2,1)S(1)} %all_to_all.17, bf16[]{:T(256)} %constant.2.clone.1), dimensions={0}, to_apply=%region_0.0 | reduce | flops 122880 | bytes 278530 | tf_op jit(solution)/shard_map/reduce_sum | solution.py:247
  (2 shorter events, 0.0 us)
Async XLA Ops:
  0.0 0.7 %copy-start.3 = (s32[8,128]{1,0:T(8,128)S(1)}, s32[8,128]{1,0:T(8,128)}, u32[]{:S(2)}) copy-start(s32[8,128]{1,0:T(8,128)} %table_ref.1) | copy-start | bytes 12292
  0.0 0.7 %copy-start.4 = (s32[8]{0:T(128)S(1)}, s32[8]{0:T(128)}, u32[]{:S(2)}) copy-start(s32[8]{0:T(128)} %param.9) | copy-start | bytes 100
  0.0 0.7 %copy-start.2 = (bf16[8,1,256]{2,0,1:T(8,128)(2,1)S(1)}, bf16[8,1,256]{2,0,1:T(8,128)(2,1)}, u32[]{:S(2)}) copy-start(bf16[8,1,256]{2,0,1:T(8,128)(2,1)} %param.7) | copy-start | bytes 12292
  0.0 0.7 %copy-start.1 = (bf16[8,512]{1,0:T(8,128)(2,1)S(1)}, bf16[8,512]{1,0:T(8,128)(2,1)}, u32[]{:S(2)}) copy-start(bf16[8,512]{1,0:T(8,128)(2,1)} %query_ref.1) | copy-start | bytes 24580
  0.0 21.0 %slice-start = ((s8[16777216]{0:T(1024)(128)(4,1)}), s8[4194304]{0:T(1024)(128)(4,1)S(1)}, s32[]{:S(2)}) async-start(s8[16777216]{0:T(1024)(128)(4,1)} %bitcast.4), calls=%async_computation.3 | async-start | bytes 8388608
  0.7 10.5 %copy-start = (bf16[1,64,128,256]{3,2,1,0:T(8,128)(2,1)S(1)}, bf16[1,64,128,256]{3,2,1,0:T(8,128)(2,1)}, u32[]{:S(2)}) copy-start(bf16[1,64,128,256]{3,2,1,0:T(8,128)(2,1)} %param.8) | copy-start | bytes 12582916
  0.7 20.2 %slice-start.1 = ((s8[16777216]{0:T(1024)(128)(4,1)}), s8[4194304]{0:T(1024)(128)(4,1)S(1)}, s32[]{:S(2)}) async-start(s8[16777216]{0:T(1024)(128)(4,1)} %bitcast.4), calls=%async_computation.4 | async-start | bytes 8388608
  0.8 20.2 %slice-start.2 = ((s8[16777216]{0:T(1024)(128)(4,1)}), s8[4194304]{0:T(1024)(128)(4,1)S(1)}, s32[]{:S(2)}) async-start(s8[16777216]{0:T(1024)(128)(4,1)} %bitcast.4), calls=%async_computation.5 | async-start | bytes 8388608
  0.8 20.2 %slice-start.3 = ((s8[16777216]{0:T(1024)(128)(4,1)}), s8[4194304]{0:T(1024)(128)(4,1)S(1)}, s32[]{:S(2)}) async-start(s8[16777216]{0:T(1024)(128)(4,1)} %bitcast.4), calls=%async_computation.6 | async-start | bytes 8388608

commit v5 on v4

--- a/solution.py
+++ b/solution.py
@@ -145,41 +145,37 @@
     summed = jnp.dot(chosen, high, preferred_element_type=F32) + jnp.dot(
         chosen, low, preferred_element_type=F32
     )
-    summed = summed.astype(BF16)
     high = [total.astype(BF16).astype(F32) for total in totals]
     low = [total - part for total, part in zip(totals, high)]
-    points = jnp.concatenate(points + points, axis=0).T
-    totals = jnp.concatenate(high + low, axis=0).T
-    wide = jnp.zeros((requests, LANES - 2 * heads), F32)
-    points = jnp.concatenate([points[:requests], wide], axis=1)
-    totals = jnp.concatenate([totals[:requests], wide], axis=1)
+    marks = jnp.concatenate(points + high + low + low, axis=0).T[:requests]
+    marks = jnp.concatenate([marks, jnp.zeros((requests, LANES - 4 * heads), F32)], axis=1)
     for g in range(requests // per_home):
         here = slice(g * per_home, (g + 1) * per_home)
         block = [summed[here, h * head_dim : (h + 1) * head_dim] for h in range(heads)]
         out_ref[g] = jnp.concatenate(
-            block + [points[here].astype(BF16), totals[here].astype(BF16)], axis=0
-        )
+            block + [marks[here]], axis=0
+        ).astype(BF16)
 
 
 def project_kernel(part_ref, state_ref, weight_ref, out_ref):
     sources, rows, head_dim = part_ref.shape
     blocks, req, own = out_ref.shape
-    heads = rows // req - 2
+    heads = rows // req - 1
     fresh = state_ref[:, head_dim:]
-    points = [part_ref[s, heads * req :, :].astype(F32)[:req] for s in range(sources)]
+    parts = [part_ref[s].astype(F32) for s in range(sources)]
+    points = [part[heads * req :] for part in parts]
     peak = fresh
     for point in points:
         peak = jnp.maximum(peak, point)
     weight = jnp.exp(fresh - peak)
     total = weight
     summed = [weight[:, h : h + 1] * state_ref[:, :head_dim] for h in range(heads)]
-    for s in range(sources):
-        factor = jnp.exp(points[s] - peak)
-        addends = part_ref[s, heads * req :, :].astype(F32)[req:]
-        total = total + factor * (addends + pltpu.roll(addends, LANES - heads, 1))
+    for part, point in zip(parts, points):
+        factor = jnp.exp(point - peak)
+        addends = pltpu.roll(point, LANES - heads, 1) + pltpu.roll(point, LANES - 2 * heads, 1)
+        total = total + factor * addends
         for h in range(heads):
-            value = part_ref[s, h * req : (h + 1) * req, :].astype(F32)
-            summed[h] = summed[h] + factor[:, h : h + 1] * value
+            summed[h] = summed[h] + factor[:, h : h + 1] * part[h * req : (h + 1) * req]
     given = jnp.concatenate(
         [summed[h] / total[:, h : h + 1] for h in range(heads)], axis=1
     ).astype(BF16)
@@ -223,7 +219,7 @@
     asked = lax.all_to_all(asked, "dp", 0, 0).reshape(requests, q_width + 2 * list_len)
     parts = pl.pallas_call(
         functools.partial(attend_kernel, scaling, n_dp, heads),
-        out_shape=jax.ShapeDtypeStruct((n_dp, req_home * (heads + 2), head_dim), BF16),
+        out_shape=jax.ShapeDtypeStruct((n_dp, req_home * (heads + 1), head_dim), BF16),
         in_specs=[vmem] * 2,
         out_specs=vmem,
         compiler_params=pltpu.CompilerParams(vmem_limit_bytes=12 * 2**20),

time: 40.5 us -> 40.4 us (level)
  no operation moved by 1% of the time
where the time goes in v5:
time: 40.4 us; the launch traced here: 40.2 us
  blocking collectives  34.7 us (86%)
  Pallas kernels  4.04 us (10%)
  local copies, waits for them, and re-layouts  0.74 us (2%)
  other arithmetic  0.65 us (2%)
    all_to_all x1, blocking collectives, body(): pieces = lax.all_to_all(partial_out, 'tensor', 0, 0)  16.2 us
    all_to_all x1, blocking collectives, body(): lax.all_to_all(asked, 'dp', 0, 0).reshape(requests, q_width + 2 * list_len)  10.4 us
    all_to_all x1, blocking collectives, body(): parts = lax.all_to_all(parts, 'dp', 0, 0)  8.09 us
    pallas_call x1, Pallas kernels, body(): pl.pallas_call(project_kernel, out_shape=jax.ShapeDtypeStruct((n_tensor,...  2.42 us
    pallas_call x1, Pallas kernels, body(): pl.pallas_call(functools.partial(attend_kernel, scaling, n_dp, heads), ou...  1.53 us

profile of v5, /device:TPU:0, one launch (start us, length us, event | category | flops | bytes accessed | tf_op | source)
XLA Modules:
  0.0 40.2 jit_solution(10101279815003405576)
XLA Ops:
  0.0 0.0 copy-start.3
  0.0 0.0 copy-start.4
  0.0 0.0 copy-start.2
  0.0 0.0 copy-start.1
  0.0 0.0 slice-start
  0.0 0.7 %copy-done.3 = s32[8,128]{1,0:T(8,128)S(1)} copy-done((s32[8,128]{1,0:T(8,128)S(1)}, s32[8,128]{1,0:T(8,128)}, u32[]{:S(2)}) %copy-start.3) | copy-done | bytes 4120
  0.7 0.0 copy-done.4
  0.7 0.0 copy-done.2
  0.7 0.0 copy-done.1
  0.7 0.0 copy-start
  0.7 0.0 slice-start.1
  0.8 0.0 slice-start.2
  0.8 0.0 slice-start.3
  0.8 0.1 ask.1
  0.8 10.4 %all_to_all.15 = bf16[8,8,768]{2,1,0:T(8,128)(2,1)S(1)} all-to-all(bf16[8,8,768]{2,1,0:T(8,128)(2,1)S(1)} %get-tuple-element.7), channel_id=1, replica_groups=mesh['dp'=8,'tensor'=16] {'dp'}, dimensions={0} | all-to-all | bytes 196608 | tf_op jit(solution)/shard_map/all_to_all | solution.py:219
  11.2 0.0 copy-done
  11.2 1.5 %attend.1 = bf16[8,40,128]{2,1,0:T(8,128)(2,1)S(1)} custom-call(bf16[64,768]{1,0:T(8,128)(2,1)S(1)} %bitcast.6, bf16[64,128,256]{2,1,0:T(8,128)(2,1)S(1)} %bitcast.7), custom_call_target="tpu_custom_call" | custom-call | flops 10000000000 | bytes 4194304 | tf_op jit(solution)/shard_map/attend/pallas_call | solution.py:220
  12.8 8.1 %all_to_all.16.part_ref = bf16[8,40,128]{2,1,0:T(8,128)(2,1)S(1)} all-to-all(bf16[8,40,128]{2,1,0:T(8,128)(2,1)S(1)} %attend.1), channel_id=1, replica_groups=mesh['dp'=8,'tensor'=16] {'dp'}, dimensions={0} | all-to-all | bytes 163840 | tf_op jit(solution)/shard_map/all_to_all | solution.py:229
  20.9 0.0 slice-done
  20.9 0.0 slice-done.1
  20.9 0.0 slice-done.2
  20.9 0.0 slice-done.3
  20.9 2.4 %project.1 = bf16[16,8,1024]{2,1,0:T(8,128)(2,1)S(1)} custom-call(bf16[8,40,128]{2,1,0:T(8,128)(2,1)S(1)} %all_to_all.16.part_ref, f32[8,256]{1,0:T(8,128)S(1)} %get-tuple-element.8.state_ref, bf16[512,16384]{1,0:T(8,128)(2,1)S(1)} %bitcast.5), custom_call_target="tpu_custom_call" | custom-call | flops 1000000000 | bytes 16777216 | tf_op jit(solution)/shard_map/project/pallas_call | solution.py:232
  23.3 16.2 %all_to_all.17 = bf16[16,8,1024]{2,1,0:T(8,128)(2,1)S(1)} all-to-all(bf16[16,8,1024]{2,1,0:T(8,128)(2,1)S(1)} %project.1), channel_id=1, replica_groups=mesh['dp'=8,'tensor'=16] {'tensor'}, dimensions={0} | all-to-all | bytes 524288 | tf_op jit(solution)/shard_map/all_to_all | solution.py:242
  39.5 0.6 %reduce_sum.12 = bf16[8,1024]{1,0:T(8,128)(2,1)} reduce(bf16[16,8,1024]{2,1,0:T(8,128)(2,1)S(1)} %all_to_all.17, bf16[]{:T(256)} %constant.2.clone.1), dimensions={0}, to_apply=%region_0.0 | reduce | flops 122880 | bytes 278530 | tf_op jit(solution)/shard_map/reduce_sum | solution.py:243
  (2 shorter events, 0.0 us)
Async XLA Ops:
  0.0 0.7 %copy-start.3 = (s32[8,128]{1,0:T(8,128)S(1)}, s32[8,128]{1,0:T(8,128)}, u32[]{:S(2)}) copy-start(s32[8,128]{1,0:T(8,128)} %table_ref.1) | copy-start | bytes 12292
  0.0 0.7 %copy-start.4 = (s32[8]{0:T(128)S(1)}, s32[8]{0:T(128)}, u32[]{:S(2)}) copy-start(s32[8]{0:T(128)} %param.9) | copy-start | bytes 100
  0.0 0.7 %copy-start.2 = (bf16[8,1,256]{2,0,1:T(8,128)(2,1)S(1)}, bf16[8,1,256]{2,0,1:T(8,128)(2,1)}, u32[]{:S(2)}) copy-start(bf16[8,1,256]{2,0,1:T(8,128)(2,1)} %param.7) | copy-start | bytes 12292
  0.0 0.7 %copy-start.1 = (bf16[8,512]{1,0:T(8,128)(2,1)S(1)}, bf16[8,512]{1,0:T(8,128)(2,1)}, u32[]{:S(2)}) copy-start(bf16[8,512]{1,0:T(8,128)(2,1)} %query_ref.1) | copy-start | bytes 24580
  0.0 20.9 %slice-start = ((s8[16777216]{0:T(1024)(128)(4,1)}), s8[4194304]{0:T(1024)(128)(4,1)S(1)}, s32[]{:S(2)}) async-start(s8[16777216]{0:T(1024)(128)(4,1)} %bitcast.4), calls=%async_computation.3 | async-start | bytes 8388608
  0.7 10.5 %copy-start = (bf16[1,64,128,256]{3,2,1,0:T(8,128)(2,1)S(1)}, bf16[1,64,128,256]{3,2,1,0:T(8,128)(2,1)}, u32[]{:S(2)}) copy-start(bf16[1,64,128,256]{3,2,1,0:T(8,128)(2,1)} %param.8) | copy-start | bytes 12582916
  0.7 20.1 %slice-start.1 = ((s8[16777216]{0:T(1024)(128)(4,1)}), s8[4194304]{0:T(1024)(128)(4,1)S(1)}, s32[]{:S(2)}) async-start(s8[16777216]{0:T(1024)(128)(4,1)} %bitcast.4), calls=%async_computation.4 | async-start | bytes 8388608
  0.8 20.1 %slice-start.2 = ((s8[16777216]{0:T(1024)(128)(4,1)}), s8[4194304]{0:T(1024)(128)(4,1)S(1)}, s32[]{:S(2)}) async-start(s8[16777216]{0:T(1024)(128)(4,1)} %bitcast.4), calls=%async_computation.5 | async-start | bytes 8388608
  0.8 20.1 %slice-start.3 = ((s8[16777216]{0:T(1024)(128)(4,1)}), s8[4194304]{0:T(1024)(128)(4,1)S(1)}, s32[]{:S(2)}) async-start(s8[16777216]{0:T(1024)(128)(4,1)} %bitcast.4), calls=%async_computation.6 | async-start | bytes 8388608

commit v6 on v5

--- a/solution.py
+++ b/solution.py
@@ -39,10 +39,9 @@
     query = query_ref[...]
     named = (table_ref[...] - PAGE_SHIFT).astype(F32).astype(BF16)
     filled = jnp.clip(length - first, 0.0, float(page_len)).astype(BF16)
-    for d in range(asked_ref.shape[0]):
-        asked_ref[d, :, :q_width] = query
-        asked_ref[d, :, q_width : q_width + list_len] = named
-        asked_ref[d, :, q_width + list_len :] = filled
+    asked_ref[:, :q_width] = query
+    asked_ref[:, q_width : q_width + list_len] = named
+    asked_ref[:, q_width + list_len :] = filled
     newest = newest_ref[...].astype(F32)
     wide = query.astype(F32)
     fresh = jnp.zeros((req, LANES), F32)
@@ -54,8 +53,13 @@
     state_ref[:, head_dim:] = fresh
 
 
+def turn_kernel(kv_ref, out_ref):
+    for p in range(kv_ref.shape[0]):
+        out_ref[p] = kv_ref[p, :, : out_ref.shape[1]].T
+
+
 def attend_kernel(scaling, homes, heads, chip_ref, *refs):
-    *other_refs, kv_ref, out_ref = refs
+    *other_refs, turned_ref, kv_ref, out_ref = refs
     asked_refs = (chip_ref, *other_refs)
     pages, page_len, width = kv_ref.shape
     head_dim = width // 2
@@ -89,19 +93,22 @@
     scores = [[] for _ in range(heads)]
     for j in range(pages // GROUP):
         here = slice(j * GROUP, (j + 1) * GROUP)
-        keys = kv_ref[here, :, :head_dim].reshape(GROUP * page_len, head_dim)
-        full = lax.dot_general(
-            jnp.concatenate([query[h][here] for h in range(heads)], axis=0).astype(BF16),
-            keys,
-            (((1,), (1,)), ((), ())),
+        asking = jnp.concatenate(
+            [
+                jnp.concatenate(
+                    [jnp.where(member == g, query[h][here], 0.0) for g in range(GROUP)], axis=1
+                )
+                for h in range(heads)
+            ],
+            axis=0,
+        ).astype(BF16)
+        group_scores = jnp.dot(
+            asking,
+            turned_ref[here].reshape(GROUP * head_dim, page_len),
             preferred_element_type=F32,
         )
         for h in range(heads):
-            rows = full[h * GROUP : (h + 1) * GROUP]
-            mine = rows[:, :page_len]
-            for g in range(1, GROUP):
-                mine = jnp.where(member == g, rows[:, g * page_len : (g + 1) * page_len], mine)
-            scores[h].append(mine)
+            scores[h].append(group_scores[h * GROUP : (h + 1) * GROUP])
     page_peak, page_total, local = [], [], []
     for h in range(heads):
         score = jnp.where(alive, jnp.concatenate(scores[h], axis=0) * scaling, FAR_BELOW)
@@ -152,7 +159,8 @@
     for g in range(requests // per_home):
         here = slice(g * per_home, (g + 1) * per_home)
         block = [summed[here, h * head_dim : (h + 1) * head_dim] for h in range(heads)]
-        out_ref[g] = jnp.concatenate(
+        core, chip = divmod(g, homes // CORES)
+        out_ref[lax.axis_index("dp") ^ (chip * CORES + core)] = jnp.concatenate(
             block + [marks[here]], axis=0
         ).astype(BF16)
 
@@ -207,7 +215,7 @@
     asked, state = pl.pallas_call(
         functools.partial(ask_kernel, scaling, page_len),
         out_shape=(
-            jax.ShapeDtypeStruct((n_dp, req_home, q_width + 2 * list_len), BF16),
+            jax.ShapeDtypeStruct((req_home, q_width + 2 * list_len), BF16),
             jax.ShapeDtypeStruct((req_home, width), F32),
         ),
         in_specs=[vmem] * 5,
@@ -216,16 +224,30 @@
         cost_estimate=pl.CostEstimate(flops=10**11, bytes_accessed=2**20, transcendentals=0),
         name="ask",
     )(begun, lengths.reshape(1, req_home), queries, new_kv[:, 0, :], page_table)
-    asked = lax.all_to_all(asked, "dp", 0, 0).reshape(requests, q_width + 2 * list_len)
+    def swap(x, mask):
+        return lax.ppermute(x, "dp", [(i, i ^ mask) for i in range(n_dp)])
+
+    near = [asked] + [swap(asked, CORES * k) for k in range(1, n_dp // CORES)]
+    near = jnp.concatenate(near, axis=0)
+    far = swap(near, 1)
+    turned = pl.pallas_call(
+        turn_kernel,
+        out_shape=jax.ShapeDtypeStruct((pool_home, head_dim, page_len), BF16),
+        in_specs=[vmem],
+        out_specs=vmem,
+        compiler_params=pltpu.CompilerParams(vmem_limit_bytes=8 * 2**20),
+        cost_estimate=pl.CostEstimate(flops=10**8, bytes_accessed=2**22, transcendentals=0),
+        name="turn",
+    )(kv_pages[0])
     parts = pl.pallas_call(
         functools.partial(attend_kernel, scaling, n_dp, heads),
         out_shape=jax.ShapeDtypeStruct((n_dp, req_home * (heads + 1), head_dim), BF16),
-        in_specs=[vmem] * 2,
+        in_specs=[vmem] * 4,
         out_specs=vmem,
         compiler_params=pltpu.CompilerParams(vmem_limit_bytes=12 * 2**20),
         cost_estimate=pl.CostEstimate(flops=10**10, bytes_accessed=2**22, transcendentals=0),
         name="attend",
-    )(asked, kv_pages[0])
+    )(near, far, turned, kv_pages[0])
     parts = lax.all_to_all(parts, "dp", 0, 0)
 
     own = features // n_tensor

time: 40.4 us -> 40.2 us (level)
  blocking collectives: 34.7 us -> 25.3 us
  waiting for transfers between devices: 0 us -> 4.76 us
  starting transfers between devices: 0 us -> 4.19 us
    all_to_all x1 -> x0, blocking collectives: 10.4 us -> none  [body(): lax.all_to_all(asked, 'dp', 0, 0).reshape(requests, q_width + 2 * list_len)]
    ppermute x0 -> x4, waiting for transfers between devices: none -> 4.76 us  [swap(): return lax.ppermute(x, 'dp', [(i, i ^ mask) for i in range(n_dp)])]
    ppermute x0 -> x4, starting transfers between devices: none -> 4.19 us  [swap(): return lax.ppermute(x, 'dp', [(i, i ^ mask) for i in range(n_dp)])]
    all_to_all x1, blocking collectives: 8.09 us -> 9.1 us  [body(): parts = lax.all_to_all(parts, 'dp', 0, 0)]
    pallas_call x0 -> x1, Pallas kernels: none -> 0.59 us  [body(): pl.pallas_call(turn_kernel, out_shape=jax.ShapeDtypeStruct((pool_home, he...]
    pallas_call x1, Pallas kernels: 1.53 us -> 1.11 us  [body(): pl.pallas_call(functools.partial(attend_kernel, scaling, n_dp, heads), ou...]
  transfers between devices with their start and end apart: 0 -> 4, of which waited for: 0 -> 3; matrix products, arithmetic and copies ran while one was open for 0% -> 0% of each run, Pallas kernels for 0% -> 1%
where the time goes in v6:
time: 40.2 us; the launch traced here: 40 us
  blocking collectives  25.3 us (63%)
  waiting for transfers between devices  4.76 us (12%)
  Pallas kernels  4.2 us (10%)
  starting transfers between devices  4.19 us (10%)
  local copies, waits for them, and re-layouts  0.77 us (2%)
  other arithmetic  0.65 us (2%)
    all_to_all x1, blocking collectives, body(): pieces = lax.all_to_all(partial_out, 'tensor', 0, 0)  16.2 us
    all_to_all x1, blocking collectives, body(): parts = lax.all_to_all(parts, 'dp', 0, 0)  9.1 us
    ppermute x4, waiting for transfers between devices, swap(): return lax.ppermute(x, 'dp', [(i, i ^ mask) for i in range(n_dp)])  4.76 us
    ppermute x4, starting transfers between devices, swap(): return lax.ppermute(x, 'dp', [(i, i ^ mask) for i in range(n_dp)])  4.19 us
    pallas_call x1, Pallas kernels, body(): pl.pallas_call(project_kernel, out_shape=jax.ShapeDtypeStruct((n_tensor,...  2.42 us
    pallas_call x1, Pallas kernels, body(): pl.pallas_call(functools.partial(attend_kernel, scaling, n_dp, heads), ou...  1.11 us
  transfers between devices with their start and end apart: 4, of which 3 were waited for; matrix products, arithmetic and copies ran while one was open for 0% of the time, Pallas kernels for 1%

profile of v6, /device:TPU:0, one launch (start us, length us, event | category | flops | bytes accessed | tf_op | source)
XLA Modules:
  0.0 40.0 jit_solution(5239722694885447899)
XLA Ops:
  0.0 0.0 copy-start.3
  0.0 0.0 copy-start.4
  0.0 0.0 copy-start.2
  0.0 0.0 copy-start.1
  0.0 0.7 %copy-done.3 = s32[8,128]{1,0:T(8,128)S(1)} copy-done((s32[8,128]{1,0:T(8,128)S(1)}, s32[8,128]{1,0:T(8,128)}, u32[]{:S(2)}) %copy-start.3) | copy-done | bytes 4120
  0.7 0.0 copy-done.4
  0.7 0.0 copy-done.2
  0.7 0.0 copy-done.1
  0.7 0.0 copy-start
  0.7 0.1 ask.1
  0.8 3.1 %collective-permute-start.2 = (bf16[8,768]{1,0:T(8,128)(2,1)S(1)}, bf16[8,768]{1,0:T(8,128)(2,1)S(1)}, u32[]{:S(2)}, u32[]{:S(2)}) collective-permute-start(bf16[8,768]{1,0:T(8,128)(2,1)S(1)} %get-tuple-element.7), channel_id=1, source_target_pairs={{0,96},{16,112},{32,64},{48,80},{64,32},{80,48},{96,0},{112,16},{1... | collective-permute-start | bytes 36872 | tf_op jit(solution)/shard_map/ppermute | solution.py:228
  3.9 0.6 %collective-permute-start.1 = (bf16[8,768]{1,0:T(8,128)(2,1)S(1)}, bf16[8,768]{1,0:T(8,128)(2,1)S(1)}, u32[]{:S(2)}, u32[]{:S(2)}) collective-permute-start(bf16[8,768]{1,0:T(8,128)(2,1)S(1)} %get-tuple-element.7), channel_id=1, source_target_pairs={{0,64},{16,80},{32,96},{48,112},{64,0},{80,16},{96,32},{112,48},{1... | collective-permute-start | bytes 36872 | tf_op jit(solution)/shard_map/ppermute | solution.py:228
  4.6 0.4 collective-permute-start
  4.9 3.3 %collective-permute-done = bf16[8,768]{1,0:T(8,128)(2,1)S(1)} collective-permute-done((bf16[8,768]{1,0:T(8,128)(2,1)S(1)}, bf16[8,768]{1,0:T(8,128)(2,1)S(1)}, u32[]{:S(2)}, u32[]{:S(2)}) %collective-permute-start) | collective-permute-done | bytes 12320 | tf_op jit(solution)/shard_map/ppermute | solution.py:228
  8.3 0.9 %collective-permute-done.1 = bf16[8,768]{1,0:T(8,128)(2,1)S(1)} collective-permute-done((bf16[8,768]{1,0:T(8,128)(2,1)S(1)}, bf16[8,768]{1,0:T(8,128)(2,1)S(1)}, u32[]{:S(2)}, u32[]{:S(2)}) %collective-permute-start.1) | collective-permute-done | bytes 12320 | tf_op jit(solution)/shard_map/ppermute | solution.py:228
  9.1 0.0 collective-permute-done.2
  9.2 0.1 collective-permute-start.3
  9.2 0.0 copy-done
  9.3 0.0 slice-start
  9.3 0.6 %turn.1.refs_1_ = bf16[64,128,128]{2,1,0:T(8,128)(2,1)S(1)} custom-call(bf16[64,128,256]{2,1,0:T(8,128)(2,1)S(1)} %bitcast.5), custom_call_target="tpu_custom_call" | custom-call | flops 100000000 | bytes 4194304 | tf_op jit(solution)/shard_map/turn/pallas_call | solution.py:233
  9.9 0.0 slice-start.1
  9.9 0.0 slice-start.2
  9.9 0.0 slice-start.3
  9.9 0.6 %collective-permute-done.3.refs_0_ = bf16[32,768]{1,0:T(8,128)(2,1)S(1)} collective-permute-done((bf16[32,768]{1,0:T(8,128)(2,1)S(1)}, bf16[32,768]{1,0:T(8,128)(2,1)S(1)}, u32[]{:S(2)}, u32[]{:S(2)}) %collective-permute-start.3) | collective-permute-done | bytes 49184 | tf_op jit(solution)/shard_map/ppermute | solution.py:228
  10.5 1.1 %attend.1 = bf16[8,40,128]{2,1,0:T(8,128)(2,1)S(1)} custom-call(bf16[32,768]{1,0:T(8,128)(2,1)S(1)} %constant_dynamic-update-slice_fusion.chip_ref, bf16[32,768]{1,0:T(8,128)(2,1)S(1)} %collective-permute-done.3.refs_0_, bf16[64,128,128]{2,1,0:T(8,128)(2,1)S(1)} %turn.1.refs_1_, bf16[64,128,256]{2,1,0:T(8,128)(2,1)S(1)} %bitcast.6), custom_call_target="tpu_custom_call" | custom-call | flops 10000000000 | bytes 4194304 | tf_op jit(solution)/shard_map/attend/pallas_call | solution.py:242
  11.6 9.1 %all_to_all.10.part_ref = bf16[8,40,128]{2,1,0:T(8,128)(2,1)S(1)} all-to-all(bf16[8,40,128]{2,1,0:T(8,128)(2,1)S(1)} %attend.1), channel_id=1, replica_groups=mesh['dp'=8,'tensor'=16] {'dp'}, dimensions={0} | all-to-all | bytes 163840 | tf_op jit(solution)/shard_map/all_to_all | solution.py:251
  20.7 0.0 slice-done
  20.7 0.0 slice-done.1
  20.7 0.0 slice-done.2
  20.7 0.0 slice-done.3
  20.7 2.4 %project.1 = bf16[16,8,1024]{2,1,0:T(8,128)(2,1)S(1)} custom-call(bf16[8,40,128]{2,1,0:T(8,128)(2,1)S(1)} %all_to_all.10.part_ref, f32[8,256]{1,0:T(8,128)S(1)} %get-tuple-element.8.state_ref, bf16[512,16384]{1,0:T(8,128)(2,1)S(1)} %bitcast.4), custom_call_target="tpu_custom_call" | custom-call | flops 1000000000 | bytes 16777216 | tf_op jit(solution)/shard_map/project/pallas_call | solution.py:254
  23.1 16.2 %all_to_all.11 = bf16[16,8,1024]{2,1,0:T(8,128)(2,1)S(1)} all-to-all(bf16[16,8,1024]{2,1,0:T(8,128)(2,1)S(1)} %project.1), channel_id=1, replica_groups=mesh['dp'=8,'tensor'=16] {'tensor'}, dimensions={0} | all-to-all | bytes 524288 | tf_op jit(solution)/shard_map/all_to_all | solution.py:264
  39.3 0.6 %reduce_sum.12 = bf16[8,1024]{1,0:T(8,128)(2,1)} reduce(bf16[16,8,1024]{2,1,0:T(8,128)(2,1)S(1)} %all_to_all.11, bf16[]{:T(256)} %constant.2.clone.1), dimensions={0}, to_apply=%region_0.0 | reduce | flops 122880 | bytes 278530 | tf_op jit(solution)/shard_map/reduce_sum | solution.py:265
  (6 shorter events, 0.0 us)
Async XLA Ops:
  0.0 0.7 %copy-start.3 = (s32[8,128]{1,0:T(8,128)S(1)}, s32[8,128]{1,0:T(8,128)}, u32[]{:S(2)}) copy-start(s32[8,128]{1,0:T(8,128)} %table_ref.1) | copy-start | bytes 12292
  0.0 0.7 %copy-start.4 = (s32[8]{0:T(128)S(1)}, s32[8]{0:T(128)}, u32[]{:S(2)}) copy-start(s32[8]{0:T(128)} %param.9) | copy-start | bytes 100
  0.0 0.7 %copy-start.2 = (bf16[8,1,256]{2,0,1:T(8,128)(2,1)S(1)}, bf16[8,1,256]{2,0,1:T(8,128)(2,1)}, u32[]{:S(2)}) copy-start(bf16[8,1,256]{2,0,1:T(8,128)(2,1)} %param.7) | copy-start | bytes 12292
  0.0 0.7 %copy-start.1 = (bf16[8,512]{1,0:T(8,128)(2,1)S(1)}, bf16[8,512]{1,0:T(8,128)(2,1)}, u32[]{:S(2)}) copy-start(bf16[8,512]{1,0:T(8,128)(2,1)} %query_ref.1) | copy-start | bytes 24580
  0.7 8.5 %copy-start = (bf16[1,64,128,256]{3,2,1,0:T(8,128)(2,1)S(1)}, bf16[1,64,128,256]{3,2,1,0:T(8,128)(2,1)}, u32[]{:S(2)}) copy-start(bf16[1,64,128,256]{3,2,1,0:T(8,128)(2,1)} %param.8) | copy-start | bytes 12582916
  0.8 8.3 %collective-permute-start.2 = (bf16[8,768]{1,0:T(8,128)(2,1)S(1)}, bf16[8,768]{1,0:T(8,128)(2,1)S(1)}, u32[]{:S(2)}, u32[]{:S(2)}) collective-permute-start(bf16[8,768]{1,0:T(8,128)(2,1)S(1)} %get-tuple-element.7), channel_id=1, source_target_pairs={{0,96},{16,112},{32,64},{48,80},{64,32},{80,48},{96,0},{112,16},{1... | collective-permute-start | bytes 36872 | tf_op jit(solution)/shard_map/ppermute | solution.py:228
  3.9 5.2 %collective-permute-start.1 = (bf16[8,768]{1,0:T(8,128)(2,1)S(1)}, bf16[8,768]{1,0:T(8,128)(2,1)S(1)}, u32[]{:S(2)}, u32[]{:S(2)}) collective-permute-start(bf16[8,768]{1,0:T(8,128)(2,1)S(1)} %get-tuple-element.7), channel_id=1, source_target_pairs={{0,64},{16,80},{32,96},{48,112},{64,0},{80,16},{96,32},{112,48},{1... | collective-permute-start | bytes 36872 | tf_op jit(solution)/shard_map/ppermute | solution.py:228
  4.6 3.7 %collective-permute-start = (bf16[8,768]{1,0:T(8,128)(2,1)S(1)}, bf16[8,768]{1,0:T(8,128)(2,1)S(1)}, u32[]{:S(2)}, u32[]{:S(2)}) collective-permute-start(bf16[8,768]{1,0:T(8,128)(2,1)S(1)} %get-tuple-element.7), channel_id=1, source_target_pairs={{0,32},{16,48},{32,0},{48,16},{64,96},{80,112},{96,64},{112,80},{1... | collective-permute-start | bytes 36872 | tf_op jit(solution)/shard_map/ppermute | solution.py:228
  9.2 1.3 %collective-permute-start.3 = (bf16[32,768]{1,0:T(8,128)(2,1)S(1)}, bf16[32,768]{1,0:T(8,128)(2,1)S(1)}, u32[]{:S(2)}, u32[]{:S(2)}) collective-permute-start(bf16[32,768]{1,0:T(8,128)(2,1)S(1)} %constant_dynamic-update-slice_fusion.chip_ref), channel_id=1, source_target_pairs={{0,16},{16,0},{32,48},{48,32},{64,80},{80,64},{96,112},{112,96},{1... | collective-permute-start | bytes 147464 | tf_op jit(solution)/shard_map/ppermute | solution.py:228
  9.3 11.4 %slice-start = ((s8[16777216]{0:T(1024)(128)(4,1)}), s8[4194304]{0:T(1024)(128)(4,1)S(1)}, s32[]{:S(2)}) async-start(s8[16777216]{0:T(1024)(128)(4,1)} %bitcast.3), calls=%async_computation.2 | async-start | bytes 8388608
  9.9 10.8 %slice-start.1 = ((s8[16777216]{0:T(1024)(128)(4,1)}), s8[4194304]{0:T(1024)(128)(4,1)S(1)}, s32[]{:S(2)}) async-start(s8[16777216]{0:T(1024)(128)(4,1)} %bitcast.3), calls=%async_computation.3 | async-start | bytes 8388608
  9.9 10.8 %slice-start.2 = ((s8[16777216]{0:T(1024)(128)(4,1)}), s8[4194304]{0:T(1024)(128)(4,1)S(1)}, s32[]{:S(2)}) async-start(s8[16777216]{0:T(1024)(128)(4,1)} %bitcast.3), calls=%async_computation.4 | async-start | bytes 8388608
  9.9 10.8 %slice-start.3 = ((s8[16777216]{0:T(1024)(128)(4,1)}), s8[4194304]{0:T(1024)(128)(4,1)S(1)}, s32[]{:S(2)}) async-start(s8[16777216]{0:T(1024)(128)(4,1)} %bitcast.3), calls=%async_computation.5 | async-start | bytes 8388608

commit v7 on v6

--- a/solution.py
+++ b/solution.py
@@ -53,13 +53,29 @@
     state_ref[:, head_dim:] = fresh
 
 
-def turn_kernel(kv_ref, out_ref):
+def search(asked_ref, first, found):
+    pages = found.shape[0]
+    q_width = asked_ref.shape[1] - 2 * LANES
+    page_id = iota((pages, LANES), 0).astype(F32) + (
+        lax.axis_index("dp") * pages - PAGE_SHIFT
+    ).astype(F32)
+    filled = asked_ref[:, q_width + LANES : q_width + 2 * LANES].astype(F32)
+    named = asked_ref[:, q_width : q_width + LANES].astype(F32)
+    named = jnp.where(filled > 0.0, named, NO_PAGE)
+    coded = filled + (iota(filled.shape, 0) + first).astype(F32) * 256.0
+    for r in range(filled.shape[0]):
+        found = jnp.where(named[r : r + 1, :] == page_id, coded[r : r + 1, :], found)
+    return found
+
+
+def turn_kernel(near_ref, kv_ref, out_ref, found_ref):
     for p in range(kv_ref.shape[0]):
         out_ref[p] = kv_ref[p, :, : out_ref.shape[1]].T
+    found_ref[...] = search(near_ref, 0, jnp.zeros(found_ref.shape, F32))
 
 
 def attend_kernel(scaling, homes, heads, chip_ref, *refs):
-    *other_refs, turned_ref, kv_ref, out_ref = refs
+    *other_refs, found_ref, turned_ref, kv_ref, out_ref = refs
     asked_refs = (chip_ref, *other_refs)
     pages, page_len, width = kv_ref.shape
     head_dim = width // 2
@@ -68,17 +84,9 @@
     per_home = requests // homes
     q_width = heads * head_dim
 
-    page_id = iota((pages, LANES), 0).astype(F32) + (
-        lax.axis_index("dp") * pages - PAGE_SHIFT
-    ).astype(F32)
-    found = jnp.zeros((pages, LANES), F32)
-    for k, asked_ref in enumerate(asked_refs):
-        filled = asked_ref[:, q_width + LANES : q_width + 2 * LANES].astype(F32)
-        named = asked_ref[:, q_width : q_width + LANES].astype(F32)
-        named = jnp.where(filled > 0.0, named, NO_PAGE)
-        coded = filled + (iota(filled.shape, 0) + k * per_chip).astype(F32) * 256.0
-        for r in range(per_chip):
-            found = jnp.where(named[r : r + 1, :] == page_id, coded[r : r + 1, :], found)
+    found = found_ref[...]
+    for k, asked_ref in enumerate(other_refs):
+        found = search(asked_ref, (k + 1) * per_chip, found)
     code = jnp.broadcast_to(jnp.sum(found, axis=1, keepdims=True), (pages, LANES))
     owner = jnp.floor(code * (1.0 / 256.0))
     alive = iota((pages, page_len), 1).astype(F32) < code - owner * 256.0
@@ -230,24 +238,27 @@
     near = [asked] + [swap(asked, CORES * k) for k in range(1, n_dp // CORES)]
     near = jnp.concatenate(near, axis=0)
     far = swap(near, 1)
-    turned = pl.pallas_call(
+    turned, found = pl.pallas_call(
         turn_kernel,
-        out_shape=jax.ShapeDtypeStruct((pool_home, head_dim, page_len), BF16),
-        in_specs=[vmem],
-        out_specs=vmem,
+        out_shape=(
+            jax.ShapeDtypeStruct((pool_home, head_dim, page_len), BF16),
+            jax.ShapeDtypeStruct((pool_home, LANES), F32),
+        ),
+        in_specs=[vmem] * 2,
+        out_specs=(vmem, vmem),
         compiler_params=pltpu.CompilerParams(vmem_limit_bytes=8 * 2**20),
         cost_estimate=pl.CostEstimate(flops=10**8, bytes_accessed=2**22, transcendentals=0),
         name="turn",
-    )(kv_pages[0])
+    )(near, kv_pages[0])
     parts = pl.pallas_call(
         functools.partial(attend_kernel, scaling, n_dp, heads),
         out_shape=jax.ShapeDtypeStruct((n_dp, req_home * (heads + 1), head_dim), BF16),
-        in_specs=[vmem] * 4,
+        in_specs=[vmem] * 5,
         out_specs=vmem,
         compiler_params=pltpu.CompilerParams(vmem_limit_bytes=12 * 2**20),
         cost_estimate=pl.CostEstimate(flops=10**10, bytes_accessed=2**22, transcendentals=0),
         name="attend",
-    )(near, far, turned, kv_pages[0])
+    )(near, far, found, turned, kv_pages[0])
     parts = lax.all_to_all(parts, "dp", 0, 0)
 
     own = features // n_tensor

time: 40.2 us -> 40.2 us (level)
  transfers between devices with their start and end apart: 4 -> 4, of which waited for: 3 -> 3; matrix products, arithmetic and copies ran while one was open for 0% -> 0% of each run, Pallas kernels for 1% -> 2%
where the time goes in v7:
time: 40.2 us; the launch traced here: 39.9 us
  blocking collectives  25.3 us (63%)
  waiting for transfers between devices  4.79 us (12%)
  Pallas kernels  4.19 us (10%)
  starting transfers between devices  4.19 us (10%)
  local copies, waits for them, and re-layouts  0.76 us (2%)
  other arithmetic  0.65 us (2%)
    all_to_all x1, blocking collectives, body(): pieces = lax.all_to_all(partial_out, 'tensor', 0, 0)  16.2 us
    all_to_all x1, blocking collectives, body(): parts = lax.all_to_all(parts, 'dp', 0, 0)  9.1 us
    ppermute x4, waiting for transfers between devices, swap(): return lax.ppermute(x, 'dp', [(i, i ^ mask) for i in range(n_dp)])  4.79 us
    ppermute x4, starting transfers between devices, swap(): return lax.ppermute(x, 'dp', [(i, i ^ mask) for i in range(n_dp)])  4.19 us
    pallas_call x1, Pallas kernels, body(): pl.pallas_call(project_kernel, out_shape=jax.ShapeDtypeStruct((n_tensor,...  2.42 us
    pallas_call x1, Pallas kernels, body(): pl.pallas_call(functools.partial(attend_kernel, scaling, n_dp, heads), ou...  1.08 us
  transfers between devices with their start and end apart: 4, of which 3 were waited for; matrix products, arithmetic and copies ran while one was open for 0% of the time, Pallas kernels for 2%

profile of v7, /device:TPU:0, one launch (start us, length us, event | category | flops | bytes accessed | tf_op | source)
XLA Modules:
  0.0 39.9 jit_solution(9860257740716158620)
XLA Ops:
  0.0 0.0 copy-start.3
  0.0 0.0 copy-start.4
  0.0 0.0 copy-start.2
  0.0 0.0 copy-start.1
  0.0 0.7 %copy-done.3 = s32[8,128]{1,0:T(8,128)S(1)} copy-done((s32[8,128]{1,0:T(8,128)S(1)}, s32[8,128]{1,0:T(8,128)}, u32[]{:S(2)}) %copy-start.3) | copy-done | bytes 4120
  0.7 0.0 copy-done.4
  0.7 0.0 copy-done.2
  0.7 0.0 copy-done.1
  0.7 0.0 copy-start
  0.7 0.1 ask.1
  0.8 3.1 %collective-permute-start.2 = (bf16[8,768]{1,0:T(8,128)(2,1)S(1)}, bf16[8,768]{1,0:T(8,128)(2,1)S(1)}, u32[]{:S(2)}, u32[]{:S(2)}) collective-permute-start(bf16[8,768]{1,0:T(8,128)(2,1)S(1)} %get-tuple-element.9), channel_id=1, source_target_pairs={{0,96},{16,112},{32,64},{48,80},{64,32},{80,48},{96,0},{112,16},{1... | collective-permute-start | bytes 36872 | tf_op jit(solution)/shard_map/ppermute | solution.py:236
  3.9 0.6 %collective-permute-start.1 = (bf16[8,768]{1,0:T(8,128)(2,1)S(1)}, bf16[8,768]{1,0:T(8,128)(2,1)S(1)}, u32[]{:S(2)}, u32[]{:S(2)}) collective-permute-start(bf16[8,768]{1,0:T(8,128)(2,1)S(1)} %get-tuple-element.9), channel_id=1, source_target_pairs={{0,64},{16,80},{32,96},{48,112},{64,0},{80,16},{96,32},{112,48},{1... | collective-permute-start | bytes 36872 | tf_op jit(solution)/shard_map/ppermute | solution.py:236
  4.6 0.4 collective-permute-start
  4.9 3.3 %collective-permute-done = bf16[8,768]{1,0:T(8,128)(2,1)S(1)} collective-permute-done((bf16[8,768]{1,0:T(8,128)(2,1)S(1)}, bf16[8,768]{1,0:T(8,128)(2,1)S(1)}, u32[]{:S(2)}, u32[]{:S(2)}) %collective-permute-start) | collective-permute-done | bytes 12320 | tf_op jit(solution)/shard_map/ppermute | solution.py:236
  8.3 0.9 %collective-permute-done.1 = bf16[8,768]{1,0:T(8,128)(2,1)S(1)} collective-permute-done((bf16[8,768]{1,0:T(8,128)(2,1)S(1)}, bf16[8,768]{1,0:T(8,128)(2,1)S(1)}, u32[]{:S(2)}, u32[]{:S(2)}) %collective-permute-start.1) | collective-permute-done | bytes 12320 | tf_op jit(solution)/shard_map/ppermute | solution.py:236
  9.1 0.0 collective-permute-done.2
  9.2 0.1 collective-permute-start.3
  9.2 0.0 copy-done
  9.3 0.6 %turn.1 = (bf16[64,128,128]{2,1,0:T(8,128)(2,1)S(1)}, f32[64,128]{1,0:T(8,128)S(1)}) custom-call(bf16[32,768]{1,0:T(8,128)(2,1)S(1)} %constant_dynamic-update-slice_fusion.near_ref.chip_ref, bf16[64,128,256]{2,1,0:T(8,128)(2,1)S(1)} %bitcast.5), custom_call_target="tpu_custom_call" | custom-call | flops 100000000 | bytes 4194304 | tf_op jit(solution)/shard_map/turn/pallas_call | solution.py:241
  9.9 0.6 %collective-permute-done.3.refs_0_ = bf16[32,768]{1,0:T(8,128)(2,1)S(1)} collective-permute-done((bf16[32,768]{1,0:T(8,128)(2,1)S(1)}, bf16[32,768]{1,0:T(8,128)(2,1)S(1)}, u32[]{:S(2)}, u32[]{:S(2)}) %collective-permute-start.3) | collective-permute-done | bytes 49184 | tf_op jit(solution)/shard_map/ppermute | solution.py:236
  10.5 0.0 slice-start
  10.5 0.0 slice-start.1
  10.5 0.0 slice-start.2
  10.5 0.0 slice-start.3
  10.5 1.1 %attend.1 = bf16[8,40,128]{2,1,0:T(8,128)(2,1)S(1)} custom-call(bf16[32,768]{1,0:T(8,128)(2,1)S(1)} %constant_dynamic-update-slice_fusion.near_ref.chip_ref, bf16[32,768]{1,0:T(8,128)(2,1)S(1)} %collective-permute-done.3.refs_0_, f32[64,128]{1,0:T(8,128)S(1)} %get-tuple-element.10.refs_1_, bf16[64,128,128]{2,1,0:T(8,128)(2,1)S(1)} %get-tuple-element.11.refs_2_, ...), custom_call_target="tpu_custom_call" | custom-call | flops 10000000000 | bytes 4194304 | tf_op jit(solution)/shard_map/attend/pallas_call | solution.py:253
  11.6 9.1 %all_to_all.10.part_ref = bf16[8,40,128]{2,1,0:T(8,128)(2,1)S(1)} all-to-all(bf16[8,40,128]{2,1,0:T(8,128)(2,1)S(1)} %attend.1), channel_id=1, replica_groups=mesh['dp'=8,'tensor'=16] {'dp'}, dimensions={0} | all-to-all | bytes 163840 | tf_op jit(solution)/shard_map/all_to_all | solution.py:262
  20.7 0.0 slice-done
  20.7 0.0 slice-done.1
  20.7 0.0 slice-done.2
  20.7 0.0 slice-done.3
  20.7 2.4 %project.1 = bf16[16,8,1024]{2,1,0:T(8,128)(2,1)S(1)} custom-call(bf16[8,40,128]{2,1,0:T(8,128)(2,1)S(1)} %all_to_all.10.part_ref, f32[8,256]{1,0:T(8,128)S(1)} %get-tuple-element.12.state_ref, bf16[512,16384]{1,0:T(8,128)(2,1)S(1)} %bitcast.4), custom_call_target="tpu_custom_call" | custom-call | flops 1000000000 | bytes 16777216 | tf_op jit(solution)/shard_map/project/pallas_call | solution.py:265
  23.1 16.2 %all_to_all.11 = bf16[16,8,1024]{2,1,0:T(8,128)(2,1)S(1)} all-to-all(bf16[16,8,1024]{2,1,0:T(8,128)(2,1)S(1)} %project.1), channel_id=1, replica_groups=mesh['dp'=8,'tensor'=16] {'tensor'}, dimensions={0} | all-to-all | bytes 524288 | tf_op jit(solution)/shard_map/all_to_all | solution.py:275
  39.3 0.6 %reduce_sum.12 = bf16[8,1024]{1,0:T(8,128)(2,1)} reduce(bf16[16,8,1024]{2,1,0:T(8,128)(2,1)S(1)} %all_to_all.11, bf16[]{:T(256)} %constant.2.clone.1), dimensions={0}, to_apply=%region_0.0 | reduce | flops 122880 | bytes 278530 | tf_op jit(solution)/shard_map/reduce_sum | solution.py:276
  (6 shorter events, 0.0 us)
Async XLA Ops:
  0.0 0.7 %copy-start.3 = (s32[8,128]{1,0:T(8,128)S(1)}, s32[8,128]{1,0:T(8,128)}, u32[]{:S(2)}) copy-start(s32[8,128]{1,0:T(8,128)} %table_ref.1) | copy-start | bytes 12292
  0.0 0.7 %copy-start.4 = (s32[8]{0:T(128)S(1)}, s32[8]{0:T(128)}, u32[]{:S(2)}) copy-start(s32[8]{0:T(128)} %param.9) | copy-start | bytes 100
  0.0 0.7 %copy-start.2 = (bf16[8,1,256]{2,0,1:T(8,128)(2,1)S(1)}, bf16[8,1,256]{2,0,1:T(8,128)(2,1)}, u32[]{:S(2)}) copy-start(bf16[8,1,256]{2,0,1:T(8,128)(2,1)} %param.7) | copy-start | bytes 12292
  0.0 0.7 %copy-start.1 = (bf16[8,512]{1,0:T(8,128)(2,1)S(1)}, bf16[8,512]{1,0:T(8,128)(2,1)}, u32[]{:S(2)}) copy-start(bf16[8,512]{1,0:T(8,128)(2,1)} %query_ref.1) | copy-start | bytes 24580
  0.7 8.5 %copy-start = (bf16[1,64,128,256]{3,2,1,0:T(8,128)(2,1)S(1)}, bf16[1,64,128,256]{3,2,1,0:T(8,128)(2,1)}, u32[]{:S(2)}) copy-start(bf16[1,64,128,256]{3,2,1,0:T(8,128)(2,1)} %param.8) | copy-start | bytes 12582916
  0.8 8.3 %collective-permute-start.2 = (bf16[8,768]{1,0:T(8,128)(2,1)S(1)}, bf16[8,768]{1,0:T(8,128)(2,1)S(1)}, u32[]{:S(2)}, u32[]{:S(2)}) collective-permute-start(bf16[8,768]{1,0:T(8,128)(2,1)S(1)} %get-tuple-element.9), channel_id=1, source_target_pairs={{0,96},{16,112},{32,64},{48,80},{64,32},{80,48},{96,0},{112,16},{1... | collective-permute-start | bytes 36872 | tf_op jit(solution)/shard_map/ppermute | solution.py:236
  3.9 5.2 %collective-permute-start.1 = (bf16[8,768]{1,0:T(8,128)(2,1)S(1)}, bf16[8,768]{1,0:T(8,128)(2,1)S(1)}, u32[]{:S(2)}, u32[]{:S(2)}) collective-permute-start(bf16[8,768]{1,0:T(8,128)(2,1)S(1)} %get-tuple-element.9), channel_id=1, source_target_pairs={{0,64},{16,80},{32,96},{48,112},{64,0},{80,16},{96,32},{112,48},{1... | collective-permute-start | bytes 36872 | tf_op jit(solution)/shard_map/ppermute | solution.py:236
  4.6 3.7 %collective-permute-start = (bf16[8,768]{1,0:T(8,128)(2,1)S(1)}, bf16[8,768]{1,0:T(8,128)(2,1)S(1)}, u32[]{:S(2)}, u32[]{:S(2)}) collective-permute-start(bf16[8,768]{1,0:T(8,128)(2,1)S(1)} %get-tuple-element.9), channel_id=1, source_target_pairs={{0,32},{16,48},{32,0},{48,16},{64,96},{80,112},{96,64},{112,80},{1... | collective-permute-start | bytes 36872 | tf_op jit(solution)/shard_map/ppermute | solution.py:236
  9.2 1.3 %collective-permute-start.3 = (bf16[32,768]{1,0:T(8,128)(2,1)S(1)}, bf16[32,768]{1,0:T(8,128)(2,1)S(1)}, u32[]{:S(2)}, u32[]{:S(2)}) collective-permute-start(bf16[32,768]{1,0:T(8,128)(2,1)S(1)} %constant_dynamic-update-slice_fusion.near_ref.chip_ref), channel_id=1, source_target_pairs={{0,16},{16,0},{32,48},{48,32},{64,80},{80,64},{96,112},{112,96},{1... | collective-permute-start | bytes 147464 | tf_op jit(solution)/shard_map/ppermute | solution.py:236
  10.5 10.2 %slice-start = ((s8[16777216]{0:T(1024)(128)(4,1)}), s8[4194304]{0:T(1024)(128)(4,1)S(1)}, s32[]{:S(2)}) async-start(s8[16777216]{0:T(1024)(128)(4,1)} %bitcast.3), calls=%async_computation.2 | async-start | bytes 8388608
  10.5 10.2 %slice-start.1 = ((s8[16777216]{0:T(1024)(128)(4,1)}), s8[4194304]{0:T(1024)(128)(4,1)S(1)}, s32[]{:S(2)}) async-start(s8[16777216]{0:T(1024)(128)(4,1)} %bitcast.3), calls=%async_computation.3 | async-start | bytes 8388608
  10.5 10.2 %slice-start.2 = ((s8[16777216]{0:T(1024)(128)(4,1)}), s8[4194304]{0:T(1024)(128)(4,1)S(1)}, s32[]{:S(2)}) async-start(s8[16777216]{0:T(1024)(128)(4,1)} %bitcast.3), calls=%async_computation.4 | async-start | bytes 8388608
  10.5 10.2 %slice-start.3 = ((s8[16777216]{0:T(1024)(128)(4,1)}), s8[4194304]{0:T(1024)(128)(4,1)S(1)}, s32[]{:S(2)}) async-start(s8[16777216]{0:T(1024)(128)(4,1)} %bitcast.3), calls=%async_computation.5 | async-start | bytes 8388608

commit v8 on v6

--- a/solution.py
+++ b/solution.py
@@ -227,7 +227,8 @@
     def swap(x, mask):
         return lax.ppermute(x, "dp", [(i, i ^ mask) for i in range(n_dp)])
 
-    near = [asked] + [swap(asked, CORES * k) for k in range(1, n_dp // CORES)]
+    moved = {k: swap(asked, CORES * k) for k in (3,2,1)}
+    near = [asked] + [moved[k] for k in range(1, n_dp // CORES)]
     near = jnp.concatenate(near, axis=0)
     far = swap(near, 1)
     turned = pl.pallas_call(

time: 40.2 us -> 40.2 us (level)
  no operation moved by 1% of the time
where the time goes in v8:
time: 40.2 us; the launch traced here: 40 us
  blocking collectives  25.3 us (63%)
  waiting for transfers between devices  4.76 us (12%)
  Pallas kernels  4.2 us (10%)
  starting transfers between devices  4.19 us (10%)
  local copies, waits for them, and re-layouts  0.77 us (2%)
  other arithmetic  0.65 us (2%)
    all_to_all x1, blocking collectives, body(): pieces = lax.all_to_all(partial_out, 'tensor', 0, 0)  16.2 us
    all_to_all x1, blocking collectives, body(): parts = lax.all_to_all(parts, 'dp', 0, 0)  9.1 us
    ppermute x4, waiting for transfers between devices, swap(): return lax.ppermute(x, 'dp', [(i, i ^ mask) for i in range(n_dp)])  4.76 us
    ppermute x4, starting transfers between devices, swap(): return lax.ppermute(x, 'dp', [(i, i ^ mask) for i in range(n_dp)])  4.19 us
    pallas_call x1, Pallas kernels, body(): pl.pallas_call(project_kernel, out_shape=jax.ShapeDtypeStruct((n_tensor,...  2.42 us
    pallas_call x1, Pallas kernels, body(): pl.pallas_call(functools.partial(attend_kernel, scaling, n_dp, heads), ou...  1.11 us
  transfers between devices with their start and end apart: 4, of which 3 were waited for; matrix products, arithmetic and copies ran while one was open for 0% of the time, Pallas kernels for 1%

profile of v8, /device:TPU:0, one launch (start us, length us, event | category | flops | bytes accessed | tf_op | source)
XLA Modules:
  0.0 40.0 jit_solution(5239722694885447899)
XLA Ops:
  0.0 0.0 copy-start.3
  0.0 0.0 copy-start.4
  0.0 0.0 copy-start.2
  0.0 0.0 copy-start.1
  0.0 0.7 %copy-done.3 = s32[8,128]{1,0:T(8,128)S(1)} copy-done((s32[8,128]{1,0:T(8,128)S(1)}, s32[8,128]{1,0:T(8,128)}, u32[]{:S(2)}) %copy-start.3) | copy-done | bytes 4120
  0.7 0.0 copy-done.4
  0.7 0.0 copy-done.2
  0.7 0.0 copy-done.1
  0.7 0.0 copy-start
  0.7 0.1 ask.1
  0.8 3.1 %collective-permute-start.2 = (bf16[8,768]{1,0:T(8,128)(2,1)S(1)}, bf16[8,768]{1,0:T(8,128)(2,1)S(1)}, u32[]{:S(2)}, u32[]{:S(2)}) collective-permute-start(bf16[8,768]{1,0:T(8,128)(2,1)S(1)} %get-tuple-element.7), channel_id=1, source_target_pairs={{0,96},{16,112},{32,64},{48,80},{64,32},{80,48},{96,0},{112,16},{1... | collective-permute-start | bytes 36872 | tf_op jit(solution)/shard_map/ppermute | solution.py:228
  3.9 0.6 %collective-permute-start.1 = (bf16[8,768]{1,0:T(8,128)(2,1)S(1)}, bf16[8,768]{1,0:T(8,128)(2,1)S(1)}, u32[]{:S(2)}, u32[]{:S(2)}) collective-permute-start(bf16[8,768]{1,0:T(8,128)(2,1)S(1)} %get-tuple-element.7), channel_id=1, source_target_pairs={{0,64},{16,80},{32,96},{48,112},{64,0},{80,16},{96,32},{112,48},{1... | collective-permute-start | bytes 36872 | tf_op jit(solution)/shard_map/ppermute | solution.py:228
  4.6 0.4 collective-permute-start
  4.9 3.3 %collective-permute-done = bf16[8,768]{1,0:T(8,128)(2,1)S(1)} collective-permute-done((bf16[8,768]{1,0:T(8,128)(2,1)S(1)}, bf16[8,768]{1,0:T(8,128)(2,1)S(1)}, u32[]{:S(2)}, u32[]{:S(2)}) %collective-permute-start) | collective-permute-done | bytes 12320 | tf_op jit(solution)/shard_map/ppermute | solution.py:228
  8.3 0.9 %collective-permute-done.1 = bf16[8,768]{1,0:T(8,128)(2,1)S(1)} collective-permute-done((bf16[8,768]{1,0:T(8,128)(2,1)S(1)}, bf16[8,768]{1,0:T(8,128)(2,1)S(1)}, u32[]{:S(2)}, u32[]{:S(2)}) %collective-permute-start.1) | collective-permute-done | bytes 12320 | tf_op jit(solution)/shard_map/ppermute | solution.py:228
  9.1 0.0 collective-permute-done.2
  9.2 0.1 collective-permute-start.3
  9.2 0.0 copy-done
  9.3 0.0 slice-start
  9.3 0.6 %turn.1.refs_1_ = bf16[64,128,128]{2,1,0:T(8,128)(2,1)S(1)} custom-call(bf16[64,128,256]{2,1,0:T(8,128)(2,1)S(1)} %bitcast.5), custom_call_target="tpu_custom_call" | custom-call | flops 100000000 | bytes 4194304 | tf_op jit(solution)/shard_map/turn/pallas_call | solution.py:234
  9.9 0.0 slice-start.1
  9.9 0.0 slice-start.2
  9.9 0.0 slice-start.3
  9.9 0.6 %collective-permute-done.3.refs_0_ = bf16[32,768]{1,0:T(8,128)(2,1)S(1)} collective-permute-done((bf16[32,768]{1,0:T(8,128)(2,1)S(1)}, bf16[32,768]{1,0:T(8,128)(2,1)S(1)}, u32[]{:S(2)}, u32[]{:S(2)}) %collective-permute-start.3) | collective-permute-done | bytes 49184 | tf_op jit(solution)/shard_map/ppermute | solution.py:228
  10.5 1.1 %attend.1 = bf16[8,40,128]{2,1,0:T(8,128)(2,1)S(1)} custom-call(bf16[32,768]{1,0:T(8,128)(2,1)S(1)} %constant_dynamic-update-slice_fusion.chip_ref, bf16[32,768]{1,0:T(8,128)(2,1)S(1)} %collective-permute-done.3.refs_0_, bf16[64,128,128]{2,1,0:T(8,128)(2,1)S(1)} %turn.1.refs_1_, bf16[64,128,256]{2,1,0:T(8,128)(2,1)S(1)} %bitcast.6), custom_call_target="tpu_custom_call" | custom-call | flops 10000000000 | bytes 4194304 | tf_op jit(solution)/shard_map/attend/pallas_call | solution.py:243
  11.6 9.1 %all_to_all.10.part_ref = bf16[8,40,128]{2,1,0:T(8,128)(2,1)S(1)} all-to-all(bf16[8,40,128]{2,1,0:T(8,128)(2,1)S(1)} %attend.1), channel_id=1, replica_groups=mesh['dp'=8,'tensor'=16] {'dp'}, dimensions={0} | all-to-all | bytes 163840 | tf_op jit(solution)/shard_map/all_to_all | solution.py:252
  20.7 0.0 slice-done
  20.7 0.0 slice-done.1
  20.7 0.0 slice-done.2
  20.7 0.0 slice-done.3
  20.7 2.4 %project.1 = bf16[16,8,1024]{2,1,0:T(8,128)(2,1)S(1)} custom-call(bf16[8,40,128]{2,1,0:T(8,128)(2,1)S(1)} %all_to_all.10.part_ref, f32[8,256]{1,0:T(8,128)S(1)} %get-tuple-element.8.state_ref, bf16[512,16384]{1,0:T(8,128)(2,1)S(1)} %bitcast.4), custom_call_target="tpu_custom_call" | custom-call | flops 1000000000 | bytes 16777216 | tf_op jit(solution)/shard_map/project/pallas_call | solution.py:255
  23.1 16.2 %all_to_all.11 = bf16[16,8,1024]{2,1,0:T(8,128)(2,1)S(1)} all-to-all(bf16[16,8,1024]{2,1,0:T(8,128)(2,1)S(1)} %project.1), channel_id=1, replica_groups=mesh['dp'=8,'tensor'=16] {'tensor'}, dimensions={0} | all-to-all | bytes 524288 | tf_op jit(solution)/shard_map/all_to_all | solution.py:265
  39.3 0.6 %reduce_sum.12 = bf16[8,1024]{1,0:T(8,128)(2,1)} reduce(bf16[16,8,1024]{2,1,0:T(8,128)(2,1)S(1)} %all_to_all.11, bf16[]{:T(256)} %constant.2.clone.1), dimensions={0}, to_apply=%region_0.0 | reduce | flops 122880 | bytes 278530 | tf_op jit(solution)/shard_map/reduce_sum | solution.py:266
  (6 shorter events, 0.0 us)
Async XLA Ops:
  0.0 0.7 %copy-start.3 = (s32[8,128]{1,0:T(8,128)S(1)}, s32[8,128]{1,0:T(8,128)}, u32[]{:S(2)}) copy-start(s32[8,128]{1,0:T(8,128)} %table_ref.1) | copy-start | bytes 12292
  0.0 0.7 %copy-start.4 = (s32[8]{0:T(128)S(1)}, s32[8]{0:T(128)}, u32[]{:S(2)}) copy-start(s32[8]{0:T(128)} %param.9) | copy-start | bytes 100
  0.0 0.7 %copy-start.2 = (bf16[8,1,256]{2,0,1:T(8,128)(2,1)S(1)}, bf16[8,1,256]{2,0,1:T(8,128)(2,1)}, u32[]{:S(2)}) copy-start(bf16[8,1,256]{2,0,1:T(8,128)(2,1)} %param.7) | copy-start | bytes 12292
  0.0 0.7 %copy-start.1 = (bf16[8,512]{1,0:T(8,128)(2,1)S(1)}, bf16[8,512]{1,0:T(8,128)(2,1)}, u32[]{:S(2)}) copy-start(bf16[8,512]{1,0:T(8,128)(2,1)} %query_ref.1) | copy-start | bytes 24580
  0.7 8.5 %copy-start = (bf16[1,64,128,256]{3,2,1,0:T(8,128)(2,1)S(1)}, bf16[1,64,128,256]{3,2,1,0:T(8,128)(2,1)}, u32[]{:S(2)}) copy-start(bf16[1,64,128,256]{3,2,1,0:T(8,128)(2,1)} %param.8) | copy-start | bytes 12582916
  0.8 8.3 %collective-permute-start.2 = (bf16[8,768]{1,0:T(8,128)(2,1)S(1)}, bf16[8,768]{1,0:T(8,128)(2,1)S(1)}, u32[]{:S(2)}, u32[]{:S(2)}) collective-permute-start(bf16[8,768]{1,0:T(8,128)(2,1)S(1)} %get-tuple-element.7), channel_id=1, source_target_pairs={{0,96},{16,112},{32,64},{48,80},{64,32},{80,48},{96,0},{112,16},{1... | collective-permute-start | bytes 36872 | tf_op jit(solution)/shard_map/ppermute | solution.py:228
  3.9 5.2 %collective-permute-start.1 = (bf16[8,768]{1,0:T(8,128)(2,1)S(1)}, bf16[8,768]{1,0:T(8,128)(2,1)S(1)}, u32[]{:S(2)}, u32[]{:S(2)}) collective-permute-start(bf16[8,768]{1,0:T(8,128)(2,1)S(1)} %get-tuple-element.7), channel_id=1, source_target_pairs={{0,64},{16,80},{32,96},{48,112},{64,0},{80,16},{96,32},{112,48},{1... | collective-permute-start | bytes 36872 | tf_op jit(solution)/shard_map/ppermute | solution.py:228
  4.6 3.7 %collective-permute-start = (bf16[8,768]{1,0:T(8,128)(2,1)S(1)}, bf16[8,768]{1,0:T(8,128)(2,1)S(1)}, u32[]{:S(2)}, u32[]{:S(2)}) collective-permute-start(bf16[8,768]{1,0:T(8,128)(2,1)S(1)} %get-tuple-element.7), channel_id=1, source_target_pairs={{0,32},{16,48},{32,0},{48,16},{64,96},{80,112},{96,64},{112,80},{1... | collective-permute-start | bytes 36872 | tf_op jit(solution)/shard_map/ppermute | solution.py:228
  9.2 1.3 %collective-permute-start.3 = (bf16[32,768]{1,0:T(8,128)(2,1)S(1)}, bf16[32,768]{1,0:T(8,128)(2,1)S(1)}, u32[]{:S(2)}, u32[]{:S(2)}) collective-permute-start(bf16[32,768]{1,0:T(8,128)(2,1)S(1)} %constant_dynamic-update-slice_fusion.chip_ref), channel_id=1, source_target_pairs={{0,16},{16,0},{32,48},{48,32},{64,80},{80,64},{96,112},{112,96},{1... | collective-permute-start | bytes 147464 | tf_op jit(solution)/shard_map/ppermute | solution.py:228
  9.3 11.4 %slice-start = ((s8[16777216]{0:T(1024)(128)(4,1)}), s8[4194304]{0:T(1024)(128)(4,1)S(1)}, s32[]{:S(2)}) async-start(s8[16777216]{0:T(1024)(128)(4,1)} %bitcast.3), calls=%async_computation.2 | async-start | bytes 8388608
  9.9 10.8 %slice-start.1 = ((s8[16777216]{0:T(1024)(128)(4,1)}), s8[4194304]{0:T(1024)(128)(4,1)S(1)}, s32[]{:S(2)}) async-start(s8[16777216]{0:T(1024)(128)(4,1)} %bitcast.3), calls=%async_computation.3 | async-start | bytes 8388608
  9.9 10.8 %slice-start.2 = ((s8[16777216]{0:T(1024)(128)(4,1)}), s8[4194304]{0:T(1024)(128)(4,1)S(1)}, s32[]{:S(2)}) async-start(s8[16777216]{0:T(1024)(128)(4,1)} %bitcast.3), calls=%async_computation.4 | async-start | bytes 8388608
  9.9 10.8 %slice-start.3 = ((s8[16777216]{0:T(1024)(128)(4,1)}), s8[4194304]{0:T(1024)(128)(4,1)S(1)}, s32[]{:S(2)}) async-start(s8[16777216]{0:T(1024)(128)(4,1)} %bitcast.3), calls=%async_computation.5 | async-start | bytes 8388608

commit v9 on v6

--- a/solution.py
+++ b/solution.py
@@ -146,12 +146,8 @@
         totals.append(total)
         scaled.append(jnp.concatenate(values[h], axis=0) * factor)
     scaled = jnp.concatenate(scaled, axis=1)
-    high = scaled.astype(BF16)
-    low = (scaled - high.astype(F32)).astype(BF16)
     chosen = picker.T[:requests].astype(BF16)
-    summed = jnp.dot(chosen, high, preferred_element_type=F32) + jnp.dot(
-        chosen, low, preferred_element_type=F32
-    )
+    summed = jnp.dot(chosen, scaled.astype(BF16), preferred_element_type=F32)
     high = [total.astype(BF16).astype(F32) for total in totals]
     low = [total - part for total, part in zip(totals, high)]
     marks = jnp.concatenate(points + high + low + low, axis=0).T[:requests]

time: 40.2 us -> 40.2 us (level)
  no operation moved by 1% of the time
where the time goes in v9:
time: 40.2 us; the launch traced here: 39.9 us
  blocking collectives  25.3 us (63%)
  waiting for transfers between devices  4.76 us (12%)
  starting transfers between devices  4.19 us (10%)
  Pallas kernels  4.18 us (10%)
  local copies, waits for them, and re-layouts  0.77 us (2%)
  other arithmetic  0.65 us (2%)
    all_to_all x1, blocking collectives, body(): pieces = lax.all_to_all(partial_out, 'tensor', 0, 0)  16.2 us
    all_to_all x1, blocking collectives, body(): parts = lax.all_to_all(parts, 'dp', 0, 0)  9.1 us
    ppermute x4, waiting for transfers between devices, swap(): return lax.ppermute(x, 'dp', [(i, i ^ mask) for i in range(n_dp)])  4.76 us
    ppermute x4, starting transfers between devices, swap(): return lax.ppermute(x, 'dp', [(i, i ^ mask) for i in range(n_dp)])  4.19 us
    pallas_call x1, Pallas kernels, body(): pl.pallas_call(project_kernel, out_shape=jax.ShapeDtypeStruct((n_tensor,...  2.42 us
    pallas_call x1, Pallas kernels, body(): pl.pallas_call(functools.partial(attend_kernel, scaling, n_dp, heads), ou...  1.08 us
  transfers between devices with their start and end apart: 4, of which 3 were waited for; matrix products, arithmetic and copies ran while one was open for 0% of the time, Pallas kernels for 1%

profile of v9, /device:TPU:0, one launch (start us, length us, event | category | flops | bytes accessed | tf_op | source)
XLA Modules:
  0.0 39.9 jit_solution(213575953079502636)
XLA Ops:
  0.0 0.0 copy-start.3
  0.0 0.0 copy-start.4
  0.0 0.0 copy-start.2
  0.0 0.0 copy-start.1
  0.0 0.7 %copy-done.3 = s32[8,128]{1,0:T(8,128)S(1)} copy-done((s32[8,128]{1,0:T(8,128)S(1)}, s32[8,128]{1,0:T(8,128)}, u32[]{:S(2)}) %copy-start.3) | copy-done | bytes 4120
  0.7 0.0 copy-done.4
  0.7 0.0 copy-done.2
  0.7 0.0 copy-done.1
  0.7 0.0 copy-start
  0.7 0.1 ask.1
  0.8 3.1 %collective-permute-start.2 = (bf16[8,768]{1,0:T(8,128)(2,1)S(1)}, bf16[8,768]{1,0:T(8,128)(2,1)S(1)}, u32[]{:S(2)}, u32[]{:S(2)}) collective-permute-start(bf16[8,768]{1,0:T(8,128)(2,1)S(1)} %get-tuple-element.7), channel_id=1, source_target_pairs={{0,96},{16,112},{32,64},{48,80},{64,32},{80,48},{96,0},{112,16},{1... | collective-permute-start | bytes 36872 | tf_op jit(solution)/shard_map/ppermute | solution.py:224
  3.9 0.6 %collective-permute-start.1 = (bf16[8,768]{1,0:T(8,128)(2,1)S(1)}, bf16[8,768]{1,0:T(8,128)(2,1)S(1)}, u32[]{:S(2)}, u32[]{:S(2)}) collective-permute-start(bf16[8,768]{1,0:T(8,128)(2,1)S(1)} %get-tuple-element.7), channel_id=1, source_target_pairs={{0,64},{16,80},{32,96},{48,112},{64,0},{80,16},{96,32},{112,48},{1... | collective-permute-start | bytes 36872 | tf_op jit(solution)/shard_map/ppermute | solution.py:224
  4.6 0.4 collective-permute-start
  4.9 3.3 %collective-permute-done = bf16[8,768]{1,0:T(8,128)(2,1)S(1)} collective-permute-done((bf16[8,768]{1,0:T(8,128)(2,1)S(1)}, bf16[8,768]{1,0:T(8,128)(2,1)S(1)}, u32[]{:S(2)}, u32[]{:S(2)}) %collective-permute-start) | collective-permute-done | bytes 12320 | tf_op jit(solution)/shard_map/ppermute | solution.py:224
  8.3 0.9 %collective-permute-done.1 = bf16[8,768]{1,0:T(8,128)(2,1)S(1)} collective-permute-done((bf16[8,768]{1,0:T(8,128)(2,1)S(1)}, bf16[8,768]{1,0:T(8,128)(2,1)S(1)}, u32[]{:S(2)}, u32[]{:S(2)}) %collective-permute-start.1) | collective-permute-done | bytes 12320 | tf_op jit(solution)/shard_map/ppermute | solution.py:224
  9.1 0.0 collective-permute-done.2
  9.2 0.1 collective-permute-start.3
  9.2 0.0 copy-done
  9.3 0.0 slice-start
  9.3 0.6 %turn.1.refs_1_ = bf16[64,128,128]{2,1,0:T(8,128)(2,1)S(1)} custom-call(bf16[64,128,256]{2,1,0:T(8,128)(2,1)S(1)} %bitcast.5), custom_call_target="tpu_custom_call" | custom-call | flops 100000000 | bytes 4194304 | tf_op jit(solution)/shard_map/turn/pallas_call | solution.py:229
  9.9 0.0 slice-start.1
  9.9 0.0 slice-start.2
  9.9 0.0 slice-start.3
  9.9 0.6 %collective-permute-done.3.refs_0_ = bf16[32,768]{1,0:T(8,128)(2,1)S(1)} collective-permute-done((bf16[32,768]{1,0:T(8,128)(2,1)S(1)}, bf16[32,768]{1,0:T(8,128)(2,1)S(1)}, u32[]{:S(2)}, u32[]{:S(2)}) %collective-permute-start.3) | collective-permute-done | bytes 49184 | tf_op jit(solution)/shard_map/ppermute | solution.py:224
  10.5 1.1 %attend.1 = bf16[8,40,128]{2,1,0:T(8,128)(2,1)S(1)} custom-call(bf16[32,768]{1,0:T(8,128)(2,1)S(1)} %constant_dynamic-update-slice_fusion.chip_ref, bf16[32,768]{1,0:T(8,128)(2,1)S(1)} %collective-permute-done.3.refs_0_, bf16[64,128,128]{2,1,0:T(8,128)(2,1)S(1)} %turn.1.refs_1_, bf16[64,128,256]{2,1,0:T(8,128)(2,1)S(1)} %bitcast.6), custom_call_target="tpu_custom_call" | custom-call | flops 10000000000 | bytes 4194304 | tf_op jit(solution)/shard_map/attend/pallas_call | solution.py:238
  11.5 9.1 %all_to_all.10.part_ref = bf16[8,40,128]{2,1,0:T(8,128)(2,1)S(1)} all-to-all(bf16[8,40,128]{2,1,0:T(8,128)(2,1)S(1)} %attend.1), channel_id=1, replica_groups=mesh['dp'=8,'tensor'=16] {'dp'}, dimensions={0} | all-to-all | bytes 163840 | tf_op jit(solution)/shard_map/all_to_all | solution.py:247
  20.6 0.0 slice-done
  20.6 0.0 slice-done.1
  20.6 0.0 slice-done.2
  20.7 0.0 slice-done.3
  20.7 2.4 %project.1 = bf16[16,8,1024]{2,1,0:T(8,128)(2,1)S(1)} custom-call(bf16[8,40,128]{2,1,0:T(8,128)(2,1)S(1)} %all_to_all.10.part_ref, f32[8,256]{1,0:T(8,128)S(1)} %get-tuple-element.8.state_ref, bf16[512,16384]{1,0:T(8,128)(2,1)S(1)} %bitcast.4), custom_call_target="tpu_custom_call" | custom-call | flops 1000000000 | bytes 16777216 | tf_op jit(solution)/shard_map/project/pallas_call | solution.py:250
  23.1 16.2 %all_to_all.11 = bf16[16,8,1024]{2,1,0:T(8,128)(2,1)S(1)} all-to-all(bf16[16,8,1024]{2,1,0:T(8,128)(2,1)S(1)} %project.1), channel_id=1, replica_groups=mesh['dp'=8,'tensor'=16] {'tensor'}, dimensions={0} | all-to-all | bytes 524288 | tf_op jit(solution)/shard_map/all_to_all | solution.py:260
  39.3 0.6 %reduce_sum.12 = bf16[8,1024]{1,0:T(8,128)(2,1)} reduce(bf16[16,8,1024]{2,1,0:T(8,128)(2,1)S(1)} %all_to_all.11, bf16[]{:T(256)} %constant.2.clone.1), dimensions={0}, to_apply=%region_0.0 | reduce | flops 122880 | bytes 278530 | tf_op jit(solution)/shard_map/reduce_sum | solution.py:261
  (6 shorter events, 0.0 us)
Async XLA Ops:
  0.0 0.7 %copy-start.3 = (s32[8,128]{1,0:T(8,128)S(1)}, s32[8,128]{1,0:T(8,128)}, u32[]{:S(2)}) copy-start(s32[8,128]{1,0:T(8,128)} %table_ref.1) | copy-start | bytes 12292
  0.0 0.7 %copy-start.4 = (s32[8]{0:T(128)S(1)}, s32[8]{0:T(128)}, u32[]{:S(2)}) copy-start(s32[8]{0:T(128)} %param.9) | copy-start | bytes 100
  0.0 0.7 %copy-start.2 = (bf16[8,1,256]{2,0,1:T(8,128)(2,1)S(1)}, bf16[8,1,256]{2,0,1:T(8,128)(2,1)}, u32[]{:S(2)}) copy-start(bf16[8,1,256]{2,0,1:T(8,128)(2,1)} %param.7) | copy-start | bytes 12292
  0.0 0.7 %copy-start.1 = (bf16[8,512]{1,0:T(8,128)(2,1)S(1)}, bf16[8,512]{1,0:T(8,128)(2,1)}, u32[]{:S(2)}) copy-start(bf16[8,512]{1,0:T(8,128)(2,1)} %query_ref.1) | copy-start | bytes 24580
  0.7 8.5 %copy-start = (bf16[1,64,128,256]{3,2,1,0:T(8,128)(2,1)S(1)}, bf16[1,64,128,256]{3,2,1,0:T(8,128)(2,1)}, u32[]{:S(2)}) copy-start(bf16[1,64,128,256]{3,2,1,0:T(8,128)(2,1)} %param.8) | copy-start | bytes 12582916
  0.8 8.3 %collective-permute-start.2 = (bf16[8,768]{1,0:T(8,128)(2,1)S(1)}, bf16[8,768]{1,0:T(8,128)(2,1)S(1)}, u32[]{:S(2)}, u32[]{:S(2)}) collective-permute-start(bf16[8,768]{1,0:T(8,128)(2,1)S(1)} %get-tuple-element.7), channel_id=1, source_target_pairs={{0,96},{16,112},{32,64},{48,80},{64,32},{80,48},{96,0},{112,16},{1... | collective-permute-start | bytes 36872 | tf_op jit(solution)/shard_map/ppermute | solution.py:224
  3.9 5.2 %collective-permute-start.1 = (bf16[8,768]{1,0:T(8,128)(2,1)S(1)}, bf16[8,768]{1,0:T(8,128)(2,1)S(1)}, u32[]{:S(2)}, u32[]{:S(2)}) collective-permute-start(bf16[8,768]{1,0:T(8,128)(2,1)S(1)} %get-tuple-element.7), channel_id=1, source_target_pairs={{0,64},{16,80},{32,96},{48,112},{64,0},{80,16},{96,32},{112,48},{1... | collective-permute-start | bytes 36872 | tf_op jit(solution)/shard_map/ppermute | solution.py:224
  4.6 3.7 %collective-permute-start = (bf16[8,768]{1,0:T(8,128)(2,1)S(1)}, bf16[8,768]{1,0:T(8,128)(2,1)S(1)}, u32[]{:S(2)}, u32[]{:S(2)}) collective-permute-start(bf16[8,768]{1,0:T(8,128)(2,1)S(1)} %get-tuple-element.7), channel_id=1, source_target_pairs={{0,32},{16,48},{32,0},{48,16},{64,96},{80,112},{96,64},{112,80},{1... | collective-permute-start | bytes 36872 | tf_op jit(solution)/shard_map/ppermute | solution.py:224
  9.2 1.3 %collective-permute-start.3 = (bf16[32,768]{1,0:T(8,128)(2,1)S(1)}, bf16[32,768]{1,0:T(8,128)(2,1)S(1)}, u32[]{:S(2)}, u32[]{:S(2)}) collective-permute-start(bf16[32,768]{1,0:T(8,128)(2,1)S(1)} %constant_dynamic-update-slice_fusion.chip_ref), channel_id=1, source_target_pairs={{0,16},{16,0},{32,48},{48,32},{64,80},{80,64},{96,112},{112,96},{1... | collective-permute-start | bytes 147464 | tf_op jit(solution)/shard_map/ppermute | solution.py:224
  9.3 11.4 %slice-start = ((s8[16777216]{0:T(1024)(128)(4,1)}), s8[4194304]{0:T(1024)(128)(4,1)S(1)}, s32[]{:S(2)}) async-start(s8[16777216]{0:T(1024)(128)(4,1)} %bitcast.3), calls=%async_computation.2 | async-start | bytes 8388608
  9.9 10.8 %slice-start.1 = ((s8[16777216]{0:T(1024)(128)(4,1)}), s8[4194304]{0:T(1024)(128)(4,1)S(1)}, s32[]{:S(2)}) async-start(s8[16777216]{0:T(1024)(128)(4,1)} %bitcast.3), calls=%async_computation.3 | async-start | bytes 8388608
  9.9 10.8 %slice-start.2 = ((s8[16777216]{0:T(1024)(128)(4,1)}), s8[4194304]{0:T(1024)(128)(4,1)S(1)}, s32[]{:S(2)}) async-start(s8[16777216]{0:T(1024)(128)(4,1)} %bitcast.3), calls=%async_computation.4 | async-start | bytes 8388608
  9.9 10.8 %slice-start.3 = ((s8[16777216]{0:T(1024)(128)(4,1)}), s8[4194304]{0:T(1024)(128)(4,1)S(1)}, s32[]{:S(2)}) async-start(s8[16777216]{0:T(1024)(128)(4,1)} %bitcast.3), calls=%async_computation.5 | async-start | bytes 8388608
